TPU v7x, 512 devices: a whole 4x4x16 slice. The times are simulated.
512 devices in a mesh: dp: 64 (over y, z), expert: 8 (over x, core).
Axes of the slice: x: 4, y: 4, z: 16, core: 2. Of those that a mesh axis runs over, the one named last changes fastest.
Arguments:
- grads: bfloat16 [256, 768, 1024], P('expert', 'dp'), may hold values from -200 to 200
- momentum: float32 [256, 768, 1024], P('expert', 'dp'), may hold values from -6 to 6
Outputs:
- update: bfloat16 [256, 768, 1024], P('expert', 'dp')
- new_momentum: float32 [256, 768, 1024], P('expert', 'dp')
All inputs are finite; a program needn't handle non-finite values.
Results may differ from a plain program's by a relative error of at most 0.017.
Values may be sent and summed in bfloat16 or wider, within the bound.
A program may use at most 64 MiB of HBM per device.

v0:
```python
from functools import partial
import math

import jax
import jax.numpy as jnp
from jax import lax
from jax.sharding import PartitionSpec as P

H = 768
D = 1024
CAP = 2
ITERS = 2


A_COEF = 3.4445
B_COEF = -4.775
C_COEF = 2.0315
MOMENT = 0.95
EPS = 1e-07


def partner(array, axis, apart):
    return lax.ppermute(array, axis, [(i, i ^ 1 << apart) for i in range(lax.axis_size(axis))])


def alternate_rows(mine, theirs, side, groups):
    count, length, width = mine.shape
    first = jnp.where(side == 0, mine, theirs).reshape(count, groups, length // groups, width)
    second = jnp.where(side == 0, theirs, mine).reshape(count, groups, length // groups, width)
    joined = jnp.stack([first, second], axis=2)
    return joined.reshape(count, 2 * length, width)


def split_schulz(incoming, side):
    groups, count, half, width = incoming.shape
    own_rows = jnp.transpose(incoming, (1, 0, 2, 3)).reshape(count, groups * half, width)
    for step in range(ITERS):
        peer_rows = partner(own_rows, "expert", 0)
        full_rows = alternate_rows(own_rows, peer_rows, side, groups)
        gram = jnp.einsum(
            "kiw,kjw->kij", own_rows, full_rows, preferred_element_type=jnp.float32
        ).astype(jnp.bfloat16)
        gram_peer = partner(gram, "expert", 0)
        gram_full = alternate_rows(gram, gram_peer, side, groups)
        square = jnp.einsum("kij,kjl->kil", gram, gram_full, preferred_element_type=jnp.float32)
        mixer = (B_COEF * gram.astype(jnp.float32) + C_COEF * square).astype(jnp.bfloat16)
        moved = jnp.einsum("kij,kjw->kiw", mixer, full_rows, preferred_element_type=jnp.float32)
        own_rows = (A_COEF * own_rows.astype(jnp.float32) + moved).astype(jnp.bfloat16)
    return jnp.transpose(own_rows.reshape(count, groups, half, width), (1, 0, 2, 3))


def assignment(matrices, groups):
    sequence = jnp.arange(2 * matrices, dtype=jnp.int32)
    pair_owner = sequence // CAP % groups
    pair_slot = sequence % CAP
    slots = CAP
    return (pair_owner, pair_slot, slots)


def local(grads, momentum):
    groups = lax.axis_size("dp")
    matrices, length, width = grads.shape
    side = lax.axis_index("expert") % 2
    gradient = grads.astype(jnp.float32)
    new_momentum = MOMENT * momentum + gradient
    nesterov = (gradient + MOMENT * new_momentum).astype(jnp.bfloat16)
    values = nesterov.astype(jnp.float32)
    partial_squares = jnp.sum(values * values, axis=(1, 2))
    totals = lax.psum(partial_squares, "dp")
    start = (values / (jnp.sqrt(totals)[:, None, None] + EPS)).astype(jnp.bfloat16)
    piece_rows = length // 2
    kept = lax.dynamic_slice_in_dim(start, side * piece_rows, piece_rows, 1)
    given = lax.dynamic_slice_in_dim(start, (1 - side) * piece_rows, piece_rows, 1)
    arrived = partner(given, "expert", 0)
    held = jnp.where(
        side == 0, jnp.concatenate([kept, arrived], 0), jnp.concatenate([arrived, kept], 0)
    )
    pair_owner, pair_slot, slots = assignment(matrices, groups)
    target = pair_owner * slots + pair_slot
    transform = partial(split_schulz, side=side)
    cells = jnp.arange(groups * slots, dtype=jnp.int32)
    selector = (target[None, :] == cells[:, None]).astype(jnp.bfloat16)
    outgoing = jnp.dot(
        selector, held.reshape(2 * matrices, piece_rows * width), preferred_element_type=jnp.float32
    )
    outgoing = outgoing.astype(jnp.bfloat16).reshape(groups, slots, piece_rows, width)
    returned = lax.all_to_all(
        transform(lax.all_to_all(outgoing, "dp", split_axis=0, concat_axis=0, tiled=True)),
        "dp",
        split_axis=0,
        concat_axis=0,
        tiled=True,
    )
    placed_back = jnp.dot(
        selector.T,
        returned.reshape(groups * slots, piece_rows * width),
        preferred_element_type=jnp.float32,
    )
    placed_back = placed_back.astype(jnp.bfloat16).reshape(2 * matrices, piece_rows, width)
    mine = lax.dynamic_slice_in_dim(placed_back, side * matrices, matrices, 0)
    theirs = lax.dynamic_slice_in_dim(placed_back, (1 - side) * matrices, matrices, 0)
    other = partner(theirs, "expert", 0)
    ortho = jnp.where(
        side == 0, jnp.concatenate([mine, other], 1), jnp.concatenate([other, mine], 1)
    )
    scale = 0.2 * math.sqrt(max(H, D))
    update = (scale * ortho.astype(jnp.float32)).astype(jnp.bfloat16)
    return (update, new_momentum)


def solution(mesh):
    in_specs = (P("expert", "dp", None), P("expert", "dp", None))
    out_specs = (P("expert", "dp", None), P("expert", "dp", None))
    return jax.shard_map(local, mesh=mesh, in_specs=in_specs, out_specs=out_specs, check_vma=False)
```

profile of v0, /device:TPU:6, one launch (start us, length us, event | category | flops | bytes accessed | tf_op | source)
XLA Modules:
  0.0 420.1 jit_solution(504047849235330035)
XLA Ops:
  0.7 2.2 fusion.17
  2.9 149.9 %psum.7 = f32[32]{0:T(128)S(1)} all-reduce(f32[32]{0:T(128)S(1)} %get-tuple-element.6), channel_id=1, replica_groups=mesh['dp'=64,'expert'=8] {'dp'}, use_global_device_ids=true, to_apply=%region_1.2 | all-reduce | flops 32 | bytes 256 | tf_op jit(solution)/shard_map/psum | solution.py:69
  158.6 3.5 reshape.71
  163.7 80.2 %all_to_all.10 = bf16[64,2,6,1024]{3,1,2,0:T(2,128)(2,1)S(1)} all-to-all(bf16[64,2,6,1024]{3,1,2,0:T(2,128)(2,1)S(1)} %copy.39), channel_id=1, replica_groups=mesh['dp'=64,'expert'=8] {'dp'}, dimensions={0} | all-to-all | bytes 3145728 | tf_op jit(solution)/shard_map/all_to_all | solution.py:88
  244.4 2.1 collective-permute-start.1
  246.5 3.2 collective-permute-done.1
  253.5 4.4 %pad_maximum_fusion = bf16[2,64,2,6,1024]{4,0,3,1,2:T(2,128)(2,1)S(1)} fusion(bf16[2,64,1,6,1024]{4,0,3,1,2:T(2,128)(2,1)S(1)} %bitcast.38, bf16[2,64,1,6,1024]{4,0,3,1,2:T(2,128)(2,1)S(1)} %bitcast.36), kind=kLoop, calls=%fused_computation.2 | loop fusion | flops 1572864 | bytes 6291456 | tf_op jit(solution)/shard_map/stack | solution.py:30
  258.0 3.7 copy.46
  265.7 2.7 collective-permute-done.2
  271.0 3.3 pad_maximum_fusion.2
  274.4 3.1 copy.51
  277.4 6.3 %add_convert_fusion.1 = bf16[2,384,1024]{2,1,0:T(8,128)(2,1)S(1)} fusion(bf16[2,768,1024]{2,0,1:T(2,128)(2,1)} %bitcast.45, bf16[2,384,768]{2,1,0:T(8,128)(2,1)} %copy-done.5, bf16[2,768,768]{2,0,1:T(2,128)(2,1)} %bitcast.48, bf16[2,384,1024]{2,0,1:T(2,128)(2,1)S(1)} %bitcast.33), kind=kOutput, calls=%fused_computation.5 | convolution fusion | flops 2120024064 | bytes 9830400 | tf_op jit(solution)/shard_map/kij,kjw->kiw/dot_general | solution.py:47
  283.7 2.5 collective-permute-start.3
  286.2 2.8 collective-permute-done.3
  292.7 4.4 %pad_maximum_fusion.1 = bf16[2,64,2,6,1024]{4,0,3,1,2:T(2,128)(2,1)S(1)} fusion(bf16[2,64,1,6,1024]{4,0,3,1,2:T(2,128)(2,1)S(1)} %bitcast.39, bf16[2,64,1,6,1024]{4,0,3,1,2:T(2,128)(2,1)S(1)} %bitcast.37), kind=kLoop, calls=%fused_computation.3 | loop fusion | flops 1572864 | bytes 6291456 | tf_op jit(solution)/shard_map/stack | solution.py:30
  297.1 3.6 copy.56
  302.6 2.1 collective-permute-start.4
  304.6 2.7 collective-permute-done.4
  309.9 3.3 pad_maximum_fusion.3
  313.3 3.1 copy.60
  316.3 6.7 %add_convert_fusion = bf16[2,384,1024]{2,1,0:T(8,128)(2,1)} fusion(bf16[2,384,1024]{2,1,0:T(8,128)(2,1)} %copy-done.3, bf16[2,768,1024]{2,0,1:T(2,128)(2,1)S(1)} %bitcast.47, bf16[2,384,768]{2,1,0:T(8,128)(2,1)} %copy-done.6, bf16[2,768,768]{2,0,1:T(2,128)(2,1)} %bitcast.49), kind=kOutput, calls=%fused_computation.4 | convolution fusion | flops 2120024064 | bytes 9830400 | tf_op jit(solution)/shard_map/kij,kjw->kiw/dot_general | solution.py:47
  323.0 4.4 %copy.63 = bf16[2,384,1024]{2,0,1:T(2,128)(2,1)} copy(bf16[2,384,1024]{2,1,0:T(8,128)(2,1)} %add_convert_fusion) | data formatting | bytes 3145728 | tf_op jit(solution)/shard_map/convert_element_type | solution.py:48
  327.4 7.3 %all-to-all-start.1 = ((bf16[64,2,6,1024]{3,1,2,0:T(2,128)(2,1)}), bf16[64,2,6,1024]{3,1,2,0:T(2,128)(2,1)S(1)}, u32[]{:S(2)}, u32[]{:S(2)}) async-start(bf16[64,2,6,1024]{3,1,2,0:T(2,128)(2,1)} %bitcast.16), calls=%async_computation.1 | async-start | bytes 3145728 | tf_op jit(solution)/shard_map/all_to_all | solution.py:87
  334.8 76.2 %all-to-all-done.1 = bf16[64,2,6,1024]{3,1,2,0:T(2,128)(2,1)S(1)} async-done(((bf16[64,2,6,1024]{3,1,2,0:T(2,128)(2,1)}), bf16[64,2,6,1024]{3,1,2,0:T(2,128)(2,1)S(1)}, u32[]{:S(2)}, u32[]{:S(2)}) %all-to-all-start.1) | async-done | bytes 1572896 | tf_op jit(solution)/shard_map/all_to_all | solution.py:87
  (49 shorter events, 35.1 us)
Async XLA Ops:
  0.6 152.1 %copy-start.2 = (bf16[32,12,1024]{2,0,1:T(8,128)(2,1)S(1)}, bf16[32,12,1024]{2,0,1:T(8,128)(2,1)}, u32[]{:S(2)}) copy-start(bf16[32,12,1024]{2,0,1:T(8,128)(2,1)} %param.2) | copy-start | bytes 2359300
  2.8 150.3 %copy-start = (f32[32,12,1024]{2,0,1:T(8,128)}, f32[32,12,1024]{2,0,1:T(8,128)S(1)}, u32[]{:S(2)}) copy-start(f32[32,12,1024]{2,0,1:T(8,128)S(1)} %get-tuple-element.7) | copy-start | bytes 4718596
  153.2 3.6 collective-permute-start
  244.4 5.3 %collective-permute-start.1 = (bf16[2,384,1024]{2,1,0:T(8,128)(2,1)S(1)}, bf16[2,384,1024]{2,1,0:T(8,128)(2,1)S(1)}, u32[]{:S(2)}, u32[]{:S(2)}) collective-permute-start(bf16[2,384,1024]{2,1,0:T(8,128)(2,1)S(1)} %copy.40), channel_id=1, source_target_pairs={{0,1},{1,0},{2,3},{3,2},{4,5},{5,4},{6,7},{7,6},{8,9},{9,8},{10,11... | collective-permute-start | bytes 4718600 | tf_op jit(solution)/shard_map/ppermute | solution.py:23
  261.6 2.0 copy-start.1
  263.6 4.9 %copy-start.5 = (bf16[2,384,768]{2,1,0:T(8,128)(2,1)}, bf16[2,384,768]{2,1,0:T(8,128)(2,1)S(1)}, u32[]{:S(2)}) copy-start(bf16[2,384,768]{2,1,0:T(8,128)(2,1)S(1)} %fusion.19) | copy-start | bytes 3538948
  263.7 4.7 %collective-permute-start.2 = (bf16[2,384,768]{2,1,0:T(8,128)(2,1)S(1)}, bf16[2,384,768]{2,1,0:T(8,128)(2,1)S(1)}, u32[]{:S(2)}, u32[]{:S(2)}) collective-permute-start(bf16[2,384,768]{2,1,0:T(8,128)(2,1)S(1)} %fusion.19), channel_id=1, source_target_pairs={{0,1},{1,0},{2,3},{3,2},{4,5},{5,4},{6,7},{7,6},{8,9},{9,8},{10,11... | collective-permute-start | bytes 3538952 | tf_op jit(solution)/shard_map/ppermute | solution.py:23
  283.7 5.7 %copy-start.3 = (bf16[2,384,1024]{2,1,0:T(8,128)(2,1)}, bf16[2,384,1024]{2,1,0:T(8,128)(2,1)S(1)}, u32[]{:S(2)}) copy-start(bf16[2,384,1024]{2,1,0:T(8,128)(2,1)S(1)} %add_convert_fusion.1) | copy-start | bytes 4718596
  283.7 5.3 %collective-permute-start.3 = (bf16[2,384,1024]{2,1,0:T(8,128)(2,1)S(1)}, bf16[2,384,1024]{2,1,0:T(8,128)(2,1)S(1)}, u32[]{:S(2)}, u32[]{:S(2)}) collective-permute-start(bf16[2,384,1024]{2,1,0:T(8,128)(2,1)S(1)} %add_convert_fusion.1), channel_id=1, source_target_pairs={{0,1},{1,0},{2,3},{3,2},{4,5},{5,4},{6,7},{7,6},{8,9},{9,8},{10,11... | collective-permute-start | bytes 4718600 | tf_op jit(solution)/shard_map/ppermute | solution.py:23
  297.1 3.7 copy-start.4
  302.6 4.9 %copy-start.6 = (bf16[2,384,768]{2,1,0:T(8,128)(2,1)}, bf16[2,384,768]{2,1,0:T(8,128)(2,1)S(1)}, u32[]{:S(2)}) copy-start(bf16[2,384,768]{2,1,0:T(8,128)(2,1)S(1)} %fusion.22) | copy-start | bytes 3538948
  302.6 4.7 %collective-permute-start.4 = (bf16[2,384,768]{2,1,0:T(8,128)(2,1)S(1)}, bf16[2,384,768]{2,1,0:T(8,128)(2,1)S(1)}, u32[]{:S(2)}, u32[]{:S(2)}) collective-permute-start(bf16[2,384,768]{2,1,0:T(8,128)(2,1)S(1)} %fusion.22), channel_id=1, source_target_pairs={{0,1},{1,0},{2,3},{3,2},{4,5},{5,4},{6,7},{7,6},{8,9},{9,8},{10,11... | collective-permute-start | bytes 3538952 | tf_op jit(solution)/shard_map/ppermute | solution.py:23
  327.4 83.5 %all-to-all-start.1 = ((bf16[64,2,6,1024]{3,1,2,0:T(2,128)(2,1)}), bf16[64,2,6,1024]{3,1,2,0:T(2,128)(2,1)S(1)}, u32[]{:S(2)}, u32[]{:S(2)}) async-start(bf16[64,2,6,1024]{3,1,2,0:T(2,128)(2,1)} %bitcast.16), calls=%async_computation.1 | async-start | bytes 3145728 | tf_op jit(solution)/shard_map/all_to_all | solution.py:87
  414.0 3.8 collective-permute-start.5
where the time goes:
time: 426 us; the launch traced here: 420 us
  blocking collectives  230 us (54%)
  waiting for transfers between devices  91.1 us (21%)
  local copies, waits for them, and re-layouts  38.9 us (9%)
  other arithmetic  20.1 us (5%)
  starting transfers between devices  19.9 us (5%)
  matrix products  18.8 us (4%)
    psum x1, blocking collectives, local(): totals = lax.psum(partial_squares, 'dp')  150 us
    all_to_all x1, blocking collectives, local(): lax.all_to_all(outgoing, 'dp', split_axis=0, concat_axis=0, tiled=True)  80.2 us
    all_to_all x1, waiting for transfers between devices, local(): lax.all_to_all(transform(lax.all_to_all(outgoing, 'dp', split_axis=0, con...  76.2 us
    another operation x4, other arithmetic, alternate_rows(): joined = jnp.stack([first, second], axis=2)  15.6 us
    ppermute x6, waiting for transfers between devices, partner(): lax.ppermute(array, axis, [(i, i ^ 1 << apart) for i in range(lax.axis_si...  14.9 us
    another operation x4, local copies, waits for them, and re-layouts, alternate_rows(): joined = jnp.stack([first, second], axis=2)  13.5 us
    dot_general x2, matrix products, split_schulz(): jnp.einsum('kij,kjw->kiw', mixer, full_rows, preferred_element_type=jnp.f...  13 us
    ppermute x6, starting transfers between devices, partner(): lax.ppermute(array, axis, [(i, i ^ 1 << apart) for i in range(lax.axis_si...  12.6 us
  transfers between devices with their start and end apart: 7, of which 7 were waited for; matrix products, arithmetic and copies ran while one was open for 0% of the time, Pallas kernels for 0%

commit v1 on v0

v1 whole, which is shorter than its diff:
```python
from functools import partial
import math

import jax
import jax.numpy as jnp
from jax import lax
from jax.experimental import pallas as pl
from jax.experimental.pallas import tpu as pltpu
from jax.sharding import PartitionSpec as P

H = 768
D = 1024
ITERS = 2

A_COEF = 3.4445
B_COEF = -4.775
C_COEF = 2.0315
MOMENT = 0.95
EPS = 1e-07

ROWS = 12
TALL = 16
MAIN = D * ROWS // TALL
EXTRA = D - MAIN
REST = TALL - ROWS
SPLITS = ROWS // REST
SIDES_Y = 4
MESH_ID = pl.DeviceIdType.MESH


def pack_rows(rows):
    tail = rows[:, MAIN:]
    below = jnp.concatenate([tail[REST * j : REST * (j + 1)] for j in range(SPLITS)], axis=1)
    return jnp.concatenate([rows[:, :MAIN], below], axis=0)


def unpack_rows(block):
    below = block[ROWS:]
    tail = jnp.concatenate(
        [below[:, EXTRA * j : EXTRA * (j + 1)] for j in range(SPLITS)], axis=0
    )
    return jnp.concatenate([block[:ROWS], tail], axis=1)


def middle_out(i, count):
    sign = 1 - 2 * (i % 2)
    return (count // 2 + sign * ((i + 1) // 2) + count) % count


def selector(plain_dim, packed_dim, shape, part):
    plain = lax.broadcasted_iota(jnp.int32, shape, plain_dim)
    packed = lax.broadcasted_iota(jnp.int32, shape, packed_dim)
    slot = (plain * 43691) >> 19
    row = plain - ROWS * slot
    if part is None:
        hit = packed == TALL * slot + row
    else:
        within = row - REST * part
        hit = (packed == TALL * slot + ROWS + within) & (within >= 0) & (within < REST)
    return jnp.where(hit, 1.0, 0.0).astype(jnp.bfloat16)


def dot(a, b):
    return jnp.dot(a, b, preferred_element_type=jnp.float32)


def dot_t(a, b):
    return lax.dot_general(a, b, (((1,), (1,)), ((), ())), preferred_element_type=jnp.float32)


def kernel(
    n_dp,
    grads_ref,
    mom_ref,
    out_ref,
    sent,
    landed,
    x0,
    x1,
    gram,
    mixer,
    away,
    home,
    sel,
    sel_t,
    sent_sem,
    landed_sem,
    away_sem,
    home_sem,
):
    n_z = n_dp // SIDES_Y
    mats = n_dp // 2
    height = ROWS * n_dp
    group = min(16, n_dp)
    plain_rows, packed_rows = ROWS * group, TALL * group
    block_rows = min(256, height)

    dp = lax.axis_index("dp")
    expert = lax.axis_index("expert")
    core = expert % 2
    y, z = dp // n_z, dp % n_z
    owns = y % 2 == core
    mine = (y // 2) * n_z + z

    def owner_of(matrix):
        return (core + 2 * (matrix // n_z)) * n_z + matrix % n_z

    barrier = pltpu.get_barrier_semaphore()

    def greet_owner(i, c):
        other = owner_of(i)

        @pl.when(other != dp)
        def _():
            pl.semaphore_signal(barrier, inc=1, device_id=(other, expert), device_id_type=MESH_ID)

        return c

    lax.fori_loop(0, mats, greet_owner, 0)

    @pl.when(owns)
    def _():
        def greet_rest(i, c):
            other = (1 - core + 2 * (i // n_z)) * n_z + i % n_z
            pl.semaphore_signal(barrier, inc=1, device_id=(other, expert), device_id_type=MESH_ID)
            return c

        lax.fori_loop(0, mats, greet_rest, 0)

    def pack_one(m, c):
        gradient = grads_ref[m].astype(jnp.float32)
        momentum = MOMENT * mom_ref[m] + gradient
        sent[m] = pack_rows(gradient + MOMENT * momentum).astype(jnp.bfloat16)
        return c

    lax.fori_loop(0, mats, pack_one, 0)

    @pl.when(owns)
    def _():
        pl.semaphore_wait(barrier, n_dp - 1)

    @pl.when(jnp.logical_not(owns))
    def _():
        pl.semaphore_wait(barrier, mats)

    def matrix_at(i):
        turn = i % (mats // 2)
        half_z = n_z // 2
        target_z = (z - z % 2 + i // (mats // 2) + 2 * middle_out(turn // 2, half_z)) % n_z
        return (turn % 2) * n_z + target_z

    def send_one(i, c):
        m = matrix_at(i)
        owner = owner_of(m)
        slot = (dp - owner + n_dp) % n_dp

        @pl.when(owner != dp)
        def _():
            pltpu.make_async_remote_copy(
                src_ref=sent.at[m],
                dst_ref=landed.at[slot],
                send_sem=sent_sem.at[m],
                recv_sem=landed_sem.at[slot],
                device_id=(owner, expert),
                device_id_type=MESH_ID,
            ).start()

        @pl.when(owner == dp)
        def _():
            pltpu.make_async_copy(sent.at[m], landed.at[0], landed_sem.at[0]).start()

        return c

    lax.fori_loop(0, mats, send_one, 0)

    @pl.when(owns)
    def _():
        for part in range(SPLITS + 1):
            which = None if part == 0 else part - 1
            sel[part] = selector(0, 1, (plain_rows, packed_rows), which)
            sel_t[part] = selector(1, 0, (packed_rows, plain_rows), which)

        def squares(slot, total):
            pltpu.make_async_copy(landed.at[slot], landed.at[slot], landed_sem.at[slot]).wait()
            values = landed[slot].astype(jnp.float32)
            return total + values * values

        total = lax.fori_loop(0, n_dp, squares, jnp.zeros((TALL, MAIN), jnp.float32))
        norm = jnp.sqrt(jnp.sum(total, axis=(0, 1), keepdims=True)) + EPS

        def unpack_group(g, c):
            block = landed[pl.ds(pl.multiple_of(g * group, group), group)]
            block = block.reshape(packed_rows, MAIN).astype(jnp.float32)
            start = (block / norm).astype(jnp.bfloat16)
            rows = pl.ds(pl.multiple_of(g * plain_rows, 16), plain_rows)
            x0[rows, :MAIN] = dot(sel[0], start).astype(jnp.bfloat16)
            tail = dot(sel[1], start[:, :EXTRA])
            for part in range(1, SPLITS):
                tail = tail + dot(sel[part + 1], start[:, EXTRA * part : EXTRA * (part + 1)])
            x0[rows, MAIN:] = tail.astype(jnp.bfloat16)
            return c

        lax.fori_loop(0, n_dp // group, unpack_group, 0)

        state = x0
        for step in range(ITERS):

            def gram_rows(r, c, state=state):
                rows = pl.ds(pl.multiple_of(r * block_rows, 16), block_rows)
                gram[rows] = dot_t(state[rows], state[...]).astype(jnp.bfloat16)
                return c

            def mixer_rows(r, c):
                rows = pl.ds(pl.multiple_of(r * block_rows, 16), block_rows)
                some = gram[rows]
                square = dot(some, gram[...])
                mixed = B_COEF * some.astype(jnp.float32) + C_COEF * square
                mixer[rows] = mixed.astype(jnp.bfloat16)
                return c

            lax.fori_loop(0, height // block_rows, gram_rows, 0)
            lax.fori_loop(0, height // block_rows, mixer_rows, 0)

            if step < ITERS - 1:

                def next_rows(r, c, state=state):
                    rows = pl.ds(pl.multiple_of(r * block_rows, 16), block_rows)
                    moved = dot(mixer[rows], state[...])
                    x1[rows] = (A_COEF * state[rows].astype(jnp.float32) + moved).astype(
                        jnp.bfloat16
                    )
                    return c

                lax.fori_loop(0, height // block_rows, next_rows, 0)
                state = x1

        scale = 0.2 * math.sqrt(max(H, D))

        def finish_group(g, c):
            rows = pl.ds(pl.multiple_of(g * plain_rows, 16), plain_rows)
            moved = dot(mixer[rows], state[...])
            ortho = (A_COEF * state[rows].astype(jnp.float32) + moved).astype(jnp.bfloat16)
            update = (scale * ortho.astype(jnp.float32)).astype(jnp.bfloat16)
            slots = pl.ds(pl.multiple_of(g * group, group), group)
            for part in range(SPLITS):
                columns = slice(EXTRA * part, EXTRA * (part + 1))
                block = dot(sel_t[0], update[:, columns]) + dot(sel_t[part + 1], update[:, MAIN:])
                away[slots, :, columns] = block.astype(jnp.bfloat16).reshape(group, TALL, EXTRA)

            def return_one(t, c):
                slot = g * group + middle_out(t, group)
                target = (dp + slot) % n_dp

                @pl.when(slot != 0)
                def _():
                    pltpu.make_async_remote_copy(
                        src_ref=away.at[slot],
                        dst_ref=home.at[mine],
                        send_sem=away_sem.at[slot],
                        recv_sem=home_sem.at[mine],
                        device_id=(target, expert),
                        device_id_type=MESH_ID,
                    ).start()

                @pl.when(slot == 0)
                def _():
                    pltpu.make_async_copy(away.at[0], home.at[mine], home_sem.at[mine]).start()

                return c

            lax.fori_loop(0, group, return_one, 0)
            return c

        lax.fori_loop(0, n_dp // group, finish_group, 0)

    def take_home(i, c):
        m = matrix_at(i)
        pltpu.make_async_copy(home.at[m], home.at[m], home_sem.at[m]).wait()
        out_ref[m] = unpack_rows(home[m].astype(jnp.float32)).astype(jnp.bfloat16)
        return c

    lax.fori_loop(0, mats, take_home, 0)

    def sent_done(m, c):
        @pl.when(owner_of(m) != dp)
        def _():
            pltpu.make_async_copy(sent.at[m], sent.at[m], sent_sem.at[m]).wait()

        return c

    lax.fori_loop(0, mats, sent_done, 0)

    @pl.when(owns)
    def _():
        def away_done(slot, c):
            pltpu.make_async_copy(away.at[slot], away.at[slot], away_sem.at[slot]).wait()
            return c

        lax.fori_loop(1, n_dp, away_done, 0)


def orthogonalized(grads, momentum, n_dp):
    mats, height = n_dp // 2, ROWS * n_dp
    group = min(16, n_dp)
    packed = lambda count: pltpu.VMEM((count, TALL, MAIN), jnp.bfloat16)
    flat = lambda *shape: pltpu.VMEM(shape, jnp.bfloat16)
    return pl.pallas_call(
        partial(kernel, n_dp),
        out_shape=jax.ShapeDtypeStruct(grads.shape, jnp.bfloat16),
        in_specs=[pl.BlockSpec(memory_space=pltpu.VMEM)] * 2,
        out_specs=pl.BlockSpec(memory_space=pltpu.VMEM),
        scratch_shapes=[
            packed(mats),
            packed(n_dp),
            flat(height, D),
            flat(height, D),
            flat(height, height),
            flat(height, height),
            packed(n_dp),
            packed(mats),
            flat(SPLITS + 1, ROWS * group, TALL * group),
            flat(SPLITS + 1, TALL * group, ROWS * group),
            pltpu.SemaphoreType.DMA((mats,)),
            pltpu.SemaphoreType.DMA((n_dp,)),
            pltpu.SemaphoreType.DMA((n_dp,)),
            pltpu.SemaphoreType.DMA((mats,)),
        ],
        compiler_params=pltpu.CompilerParams(
            collective_id=0, has_side_effects=True, vmem_limit_bytes=40 * 1024 * 1024
        ),
        cost_estimate=pl.CostEstimate(
            flops=8 * height * height * D, bytes_accessed=8 * grads.size, transcendentals=0
        ),
    )(grads, momentum)


def local(grads, momentum):
    n_dp = lax.axis_size("dp")
    update = orthogonalized(grads, momentum, n_dp)
    new_momentum = MOMENT * momentum + grads.astype(jnp.float32)
    return (update, new_momentum)


def solution(mesh):
    in_specs = (P("expert", "dp", None), P("expert", "dp", None))
    out_specs = (P("expert", "dp", None), P("expert", "dp", None))
    return jax.shard_map(local, mesh=mesh, in_specs=in_specs, out_specs=out_specs, check_vma=False)
```

time: 426 us -> 107 us (0.25); the launches traced: 420 us -> 107 us
  blocking collectives: 230 us -> 0 us
  Pallas kernels: 0 us -> 101 us
  waiting for transfers between devices: 91.1 us -> 0 us
  local copies, waits for them, and re-layouts: 38.9 us -> 4.3 us
  starting transfers between devices: 19.9 us -> 0 us
  matrix products: 18.8 us -> 0 us
  other arithmetic: 20.1 us -> 1.41 us
    psum x1 -> x0, blocking collectives: 150 us -> none  [local(): totals = lax.psum(partial_squares, 'dp')]
    pallas_call x0 -> x1, Pallas kernels: none -> 101 us  [orthogonalized(): pl.pallas_call(partial(kernel, n_dp), out_shape=jax.ShapeDtypeStruct(grad...]
    all_to_all x1 -> x0, blocking collectives: 80.2 us -> none  [local(): lax.all_to_all(outgoing, 'dp', split_axis=0, concat_axis=0, tiled=True)]
    all_to_all x1 -> x0, waiting for transfers between devices: 76.2 us -> none  [local(): lax.all_to_all(transform(lax.all_to_all(outgoing, 'dp', split_axis=0, con...]
    dot_general x6 -> x0, matrix products: 18.8 us -> none  [the longest x2 13 us: split_schulz(): jnp.einsum('kij,kjw->kiw', mixer, full_rows, preferred_element_type=jnp.f...]
    another operation x4 -> x0, other arithmetic: 15.6 us -> none  [alternate_rows(): joined = jnp.stack([first, second], axis=2)]
    ppermute x6 -> x0, waiting for transfers between devices: 14.9 us -> none  [partner(): lax.ppermute(array, axis, [(i, i ^ 1 << apart) for i in range(lax.axis_si...]
    another operation x4 -> x0, local copies, waits for them, and re-layouts: 13.5 us -> none  [alternate_rows(): joined = jnp.stack([first, second], axis=2)]
  transfers between devices with their start and end apart: 7 -> 0, of which waited for: 7 -> 0; matrix products, arithmetic and copies ran while one was open for 0% -> 0% of each run, Pallas kernels for 0% -> 0%
where the time goes in v1:
time: 107 us
  Pallas kernels  101 us (94%)
  local copies, waits for them, and re-layouts  4.3 us (4%)
  other arithmetic  1.41 us (1%)
    pallas_call x1, Pallas kernels, orthogonalized(): pl.pallas_call(partial(kernel, n_dp), out_shape=jax.ShapeDtypeStruct(grad...  101 us
    unnamed x7, local copies, waits for them, and re-layouts  4.3 us

profile of v1, /device:TPU:6, one launch (start us, length us, event | category | flops | bytes accessed | tf_op | source)
XLA Modules:
  0.0 106.9 jit_solution(10035573364978521067)
XLA Ops:
  0.6 0.0 copy-start.1
  0.6 2.4 %copy.5.mom_ref = f32[32,12,1024]{2,1,0:T(8,128)S(1)} copy(f32[32,12,1024]{2,0,1:T(8,128)} %param.3) | data formatting | bytes 3145728 | tf_op args[1]
  3.1 0.0 copy-done.1
  3.1 0.4 copy.4.grads_ref
  3.5 100.5 %shard_map.41 = bf16[32,12,1024]{2,1,0:T(8,128)(2,1)S(1)} custom-call(bf16[32,12,1024]{2,1,0:T(8,128)(2,1)S(1)} %copy.4.grads_ref, f32[32,12,1024]{2,1,0:T(8,128)S(1)} %copy.5.mom_ref), custom_call_target="tpu_custom_call" | custom-call | flops 4831838208 | bytes 3145728 | tf_op jit(solution)/shard_map/pallas_call | solution.py:307
  104.0 0.0 copy-start
  104.1 1.3 %copy.6 = bf16[32,12,1024]{2,0,1:T(8,128)(2,1)} copy(bf16[32,12,1024]{2,1,0:T(8,128)(2,1)S(1)} %shard_map.41) | data formatting | bytes 1572864
  105.4 0.1 copy-done
  105.5 1.4 %convert_add_fusion = f32[32,12,1024]{2,0,1:T(8,128)} fusion(bf16[32,12,1024]{2,0,1:T(8,128)(2,1)S(1)} %copy-done.1, f32[32,12,1024]{2,0,1:T(8,128)S(1)} %copy-done), kind=kLoop, calls=%fused_computation | loop fusion | flops 1179648 | bytes 3932160 | tf_op jit(solution)/shard_map/add | solution.py:340
Async XLA Ops:
  0.6 2.4 %copy-start.1 = (bf16[32,12,1024]{2,0,1:T(8,128)(2,1)S(1)}, bf16[32,12,1024]{2,0,1:T(8,128)(2,1)}, u32[]{:S(2)}) copy-start(bf16[32,12,1024]{2,0,1:T(8,128)(2,1)} %param.2) | copy-start | bytes 2359300
  104.0 1.4 %copy-start = (f32[32,12,1024]{2,0,1:T(8,128)S(1)}, f32[32,12,1024]{2,0,1:T(8,128)}, u32[]{:S(2)}) copy-start(f32[32,12,1024]{2,0,1:T(8,128)} %param.3) | copy-start | bytes 4718596

commit v2 on v1

--- a/solution.py
+++ b/solution.py
@@ -171,7 +171,19 @@
 
         return c
 
-    lax.fori_loop(0, mats, send_one, 0)
+    def send_done(i, c):
+        m = matrix_at(i)
+
+        @pl.when(owner_of(m) != dp)
+        def _():
+            pltpu.make_async_copy(sent.at[m], sent.at[m], sent_sem.at[m]).wait()
+
+        return c
+
+    half = mats // 2
+    lax.fori_loop(0, half, send_one, 0)
+    lax.fori_loop(0, half - half // 4, send_done, 0)
+    lax.fori_loop(half, mats, send_one, 0)
 
     @pl.when(owns)
     def _():
@@ -281,14 +293,7 @@
 
     lax.fori_loop(0, mats, take_home, 0)
 
-    def sent_done(m, c):
-        @pl.when(owner_of(m) != dp)
-        def _():
-            pltpu.make_async_copy(sent.at[m], sent.at[m], sent_sem.at[m]).wait()
-
-        return c
-
-    lax.fori_loop(0, mats, sent_done, 0)
+    lax.fori_loop(half - half // 4, mats, send_done, 0)
 
     @pl.when(owns)
     def _():

time: 107 us -> 108 us (level)
    pallas_call x1, Pallas kernels: 101 us -> 102 us  [orthogonalized(): pl.pallas_call(partial(kernel, n_dp), out_shape=jax.ShapeDtypeStruct(grad...]
where the time goes in v2:
time: 108 us
  Pallas kernels  102 us (94%)
  local copies, waits for them, and re-layouts  4.3 us (4%)
  other arithmetic  1.41 us (1%)
    pallas_call x1, Pallas kernels, orthogonalized(): pl.pallas_call(partial(kernel, n_dp), out_shape=jax.ShapeDtypeStruct(grad...  102 us
    unnamed x7, local copies, waits for them, and re-layouts  4.3 us

profile of v2, /device:TPU:6, one launch (start us, length us, event | category | flops | bytes accessed | tf_op | source)
XLA Modules:
  0.0 108.3 jit_solution(9223248693586555804)
XLA Ops:
  0.6 0.0 copy-start.1
  0.6 2.4 %copy.5.mom_ref = f32[32,12,1024]{2,1,0:T(8,128)S(1)} copy(f32[32,12,1024]{2,0,1:T(8,128)} %param.3) | data formatting | bytes 3145728 | tf_op args[1]
  3.1 0.0 copy-done.1
  3.1 0.4 copy.4.grads_ref
  3.5 101.9 %shard_map.41 = bf16[32,12,1024]{2,1,0:T(8,128)(2,1)S(1)} custom-call(bf16[32,12,1024]{2,1,0:T(8,128)(2,1)S(1)} %copy.4.grads_ref, f32[32,12,1024]{2,1,0:T(8,128)S(1)} %copy.5.mom_ref), custom_call_target="tpu_custom_call" | custom-call | flops 4831838208 | bytes 3145728 | tf_op jit(solution)/shard_map/pallas_call | solution.py:312
  105.4 0.0 copy-start
  105.4 1.3 %copy.6 = bf16[32,12,1024]{2,0,1:T(8,128)(2,1)} copy(bf16[32,12,1024]{2,1,0:T(8,128)(2,1)S(1)} %shard_map.41) | data formatting | bytes 1572864
  106.7 0.1 copy-done
  106.8 1.4 %convert_add_fusion = f32[32,12,1024]{2,0,1:T(8,128)} fusion(bf16[32,12,1024]{2,0,1:T(8,128)(2,1)S(1)} %copy-done.1, f32[32,12,1024]{2,0,1:T(8,128)S(1)} %copy-done), kind=kLoop, calls=%fused_computation | loop fusion | flops 1179648 | bytes 3932160 | tf_op jit(solution)/shard_map/add | solution.py:345
Async XLA Ops:
  0.6 2.4 %copy-start.1 = (bf16[32,12,1024]{2,0,1:T(8,128)(2,1)S(1)}, bf16[32,12,1024]{2,0,1:T(8,128)(2,1)}, u32[]{:S(2)}) copy-start(bf16[32,12,1024]{2,0,1:T(8,128)(2,1)} %param.2) | copy-start | bytes 2359300
  105.4 1.4 %copy-start = (f32[32,12,1024]{2,0,1:T(8,128)S(1)}, f32[32,12,1024]{2,0,1:T(8,128)}, u32[]{:S(2)}) copy-start(f32[32,12,1024]{2,0,1:T(8,128)} %param.3) | copy-start | bytes 4718596

commit v3 on v1

--- a/solution.py
+++ b/solution.py
@@ -83,17 +83,23 @@
     home,
     sel,
     sel_t,
+    via,
+    back,
     sent_sem,
     landed_sem,
     away_sem,
     home_sem,
+    via_sem,
+    via_sent_sem,
+    back_sem,
+    back_sent_sem,
 ):
     n_z = n_dp // SIDES_Y
     mats = n_dp // 2
     height = ROWS * n_dp
     group = min(16, n_dp)
     plain_rows, packed_rows = ROWS * group, TALL * group
-    block_rows = min(256, height)
+    block_rows = 256 if height % 256 == 0 else plain_rows
 
     dp = lax.axis_index("dp")
     expert = lax.axis_index("expert")
@@ -149,20 +155,39 @@
         target_z = (z - z % 2 + i // (mats // 2) + 2 * middle_out(turn // 2, half_z)) % n_z
         return (turn % 2) * n_z + target_z
 
+    quarter = n_z // 4
+
+    def copy_to(target, src, dst, send_sem, recv_sem):
+        return pltpu.make_async_remote_copy(
+            src_ref=src,
+            dst_ref=dst,
+            send_sem=send_sem,
+            recv_sem=recv_sem,
+            device_id=(target, expert),
+            device_id_type=MESH_ID,
+        )
+
+    def relay_z(rises):
+        return (z + jnp.where(rises, quarter, n_z - quarter)) % n_z
+
+    def send_far(turn, c):
+        m = turn * n_z + (z + n_z // 2) % n_z
+        relay = (core + 2 * turn) * n_z + relay_z((z // 2 + turn) % 2 == 0)
+        copy_to(relay, sent.at[m], via.at[y], sent_sem.at[m], via_sem.at[y]).start()
+        return c
+
+    lax.fori_loop(0, 2, send_far, 0)
+
     def send_one(i, c):
         m = matrix_at(i)
         owner = owner_of(m)
         slot = (dp - owner + n_dp) % n_dp
-
-        @pl.when(owner != dp)
+        far = (owner - dp + n_dp) % n_z == n_z // 2
+
+        @pl.when((owner != dp) & jnp.logical_not(far))
         def _():
-            pltpu.make_async_remote_copy(
-                src_ref=sent.at[m],
-                dst_ref=landed.at[slot],
-                send_sem=sent_sem.at[m],
-                recv_sem=landed_sem.at[slot],
-                device_id=(owner, expert),
-                device_id_type=MESH_ID,
+            copy_to(
+                owner, sent.at[m], landed.at[slot], sent_sem.at[m], landed_sem.at[slot]
             ).start()
 
         @pl.when(owner == dp)
@@ -171,7 +196,26 @@
 
         return c
 
-    lax.fori_loop(0, mats, send_one, 0)
+    lax.fori_loop(0, mats // 4, send_one, 0)
+
+    @pl.when(owns)
+    def _():
+        rises = ((z + n_z - quarter) // 2 + y // 2) % 2 == 0
+        source_z = (z + jnp.where(rises, n_z - quarter, quarter)) % n_z
+        owner = y * n_z + relay_z(rises)
+
+        def pass_on(source_y, c):
+            slot = (source_y * n_z + source_z - owner + n_dp) % n_dp
+            block = via.at[source_y]
+            pltpu.make_async_copy(block, block, via_sem.at[source_y]).wait()
+            copy_to(
+                owner, block, landed.at[slot], via_sent_sem.at[source_y], landed_sem.at[slot]
+            ).start()
+            return c
+
+        lax.fori_loop(0, SIDES_Y, pass_on, 0)
+
+    lax.fori_loop(mats // 4, mats, send_one, 0)
 
     @pl.when(owns)
     def _():
@@ -250,16 +294,24 @@
             def return_one(t, c):
                 slot = g * group + middle_out(t, group)
                 target = (dp + slot) % n_dp
-
-                @pl.when(slot != 0)
+                target_y = target // n_z
+                far = slot % n_z == n_z // 2
+
+                @pl.when((slot != 0) & jnp.logical_not(far))
                 def _():
-                    pltpu.make_async_remote_copy(
-                        src_ref=away.at[slot],
-                        dst_ref=home.at[mine],
-                        send_sem=away_sem.at[slot],
-                        recv_sem=home_sem.at[mine],
-                        device_id=(target, expert),
-                        device_id_type=MESH_ID,
+                    copy_to(
+                        target, away.at[slot], home.at[mine], away_sem.at[slot], home_sem.at[mine]
+                    ).start()
+
+                @pl.when(far)
+                def _():
+                    relay = y * n_z + relay_z((z // 2 + target_y) % 2 == 0)
+                    copy_to(
+                        relay,
+                        away.at[slot],
+                        back.at[target_y],
+                        away_sem.at[slot],
+                        back_sem.at[target_y],
                     ).start()
 
                 @pl.when(slot == 0)
@@ -272,6 +324,20 @@
             return c
 
         lax.fori_loop(0, n_dp // group, finish_group, 0)
+
+        def pass_back(target_y, c):
+            rises = ((z + n_z - quarter) // 2 + target_y) % 2 == 0
+            owner_z = (z + jnp.where(rises, n_z - quarter, quarter)) % n_z
+            m = (y // 2) * n_z + owner_z
+            target = target_y * n_z + relay_z(rises)
+            block = back.at[target_y]
+            pltpu.make_async_copy(block, block, back_sem.at[target_y]).wait()
+            copy_to(
+                target, block, home.at[m], back_sent_sem.at[target_y], home_sem.at[m]
+            ).start()
+            return c
+
+        lax.fori_loop(0, SIDES_Y, pass_back, 0)
 
     def take_home(i, c):
         m = matrix_at(i)
@@ -297,6 +363,13 @@
             return c
 
         lax.fori_loop(1, n_dp, away_done, 0)
+
+        def passed(side, c):
+            pltpu.make_async_copy(via.at[side], via.at[side], via_sent_sem.at[side]).wait()
+            pltpu.make_async_copy(back.at[side], back.at[side], back_sent_sem.at[side]).wait()
+            return c
+
+        lax.fori_loop(0, SIDES_Y, passed, 0)
 
 
 def orthogonalized(grads, momentum, n_dp):
@@ -320,10 +393,13 @@
             packed(mats),
             flat(SPLITS + 1, ROWS * group, TALL * group),
             flat(SPLITS + 1, TALL * group, ROWS * group),
+            packed(SIDES_Y),
+            packed(SIDES_Y),
             pltpu.SemaphoreType.DMA((mats,)),
             pltpu.SemaphoreType.DMA((n_dp,)),
             pltpu.SemaphoreType.DMA((n_dp,)),
             pltpu.SemaphoreType.DMA((mats,)),
+            *[pltpu.SemaphoreType.DMA((SIDES_Y,))] * 4,
         ],
         compiler_params=pltpu.CompilerParams(
             collective_id=0, has_side_effects=True, vmem_limit_bytes=40 * 1024 * 1024

time: 107 us -> 110 us (1.028)
  Pallas kernels: 101 us -> 103 us
    pallas_call x1, Pallas kernels: 101 us -> 103 us  [orthogonalized(): pl.pallas_call(partial(kernel, n_dp), out_shape=jax.ShapeDtypeStruct(grad...]
where the time goes in v3:
time: 110 us
  Pallas kernels  103 us (94%)
  local copies, waits for them, and re-layouts  4.3 us (4%)
  other arithmetic  1.41 us (1%)
    pallas_call x1, Pallas kernels, orthogonalized(): pl.pallas_call(partial(kernel, n_dp), out_shape=jax.ShapeDtypeStruct(grad...  103 us
    unnamed x7, local copies, waits for them, and re-layouts  4.3 us

profile of v3, /device:TPU:6, one launch (start us, length us, event | category | flops | bytes accessed | tf_op | source)
XLA Modules:
  0.0 109.7 jit_solution(8284031363819469497)
XLA Ops:
  0.6 0.0 copy-start.1
  0.6 2.4 %copy.5.mom_ref = f32[32,12,1024]{2,1,0:T(8,128)S(1)} copy(f32[32,12,1024]{2,0,1:T(8,128)} %param.3) | data formatting | bytes 3145728 | tf_op args[1]
  3.1 0.0 copy-done.1
  3.1 0.4 copy.4.grads_ref
  3.5 103.3 %shard_map.41 = bf16[32,12,1024]{2,1,0:T(8,128)(2,1)S(1)} custom-call(bf16[32,12,1024]{2,1,0:T(8,128)(2,1)S(1)} %copy.4.grads_ref, f32[32,12,1024]{2,1,0:T(8,128)S(1)} %copy.5.mom_ref), custom_call_target="tpu_custom_call" | custom-call | flops 4831838208 | bytes 3145728 | tf_op jit(solution)/shard_map/pallas_call | solution.py:380
  106.9 0.0 copy-start
  106.9 1.3 %copy.6 = bf16[32,12,1024]{2,0,1:T(8,128)(2,1)} copy(bf16[32,12,1024]{2,1,0:T(8,128)(2,1)S(1)} %shard_map.41) | data formatting | bytes 1572864
  108.2 0.1 copy-done
  108.3 1.4 %convert_add_fusion = f32[32,12,1024]{2,0,1:T(8,128)} fusion(bf16[32,12,1024]{2,0,1:T(8,128)(2,1)S(1)} %copy-done.1, f32[32,12,1024]{2,0,1:T(8,128)S(1)} %copy-done), kind=kLoop, calls=%fused_computation | loop fusion | flops 1179648 | bytes 3932160 | tf_op jit(solution)/shard_map/add | solution.py:416
Async XLA Ops:
  0.6 2.4 %copy-start.1 = (bf16[32,12,1024]{2,0,1:T(8,128)(2,1)S(1)}, bf16[32,12,1024]{2,0,1:T(8,128)(2,1)}, u32[]{:S(2)}) copy-start(bf16[32,12,1024]{2,0,1:T(8,128)(2,1)} %param.2) | copy-start | bytes 2359300
  106.9 1.4 %copy-start = (f32[32,12,1024]{2,0,1:T(8,128)S(1)}, f32[32,12,1024]{2,0,1:T(8,128)}, u32[]{:S(2)}) copy-start(f32[32,12,1024]{2,0,1:T(8,128)} %param.3) | copy-start | bytes 4718596

commit v4 on v1

--- a/solution.py
+++ b/solution.py
@@ -25,6 +25,7 @@
 REST = TALL - ROWS
 SPLITS = ROWS // REST
 SIDES_Y = 4
+BATCHES = 4
 MESH_ID = pl.DeviceIdType.MESH
 
 
@@ -93,7 +94,7 @@
     height = ROWS * n_dp
     group = min(16, n_dp)
     plain_rows, packed_rows = ROWS * group, TALL * group
-    block_rows = min(256, height)
+    block_rows = 256 if height % 256 == 0 else plain_rows
 
     dp = lax.axis_index("dp")
     expert = lax.axis_index("expert")
@@ -144,10 +145,10 @@
         pl.semaphore_wait(barrier, mats)
 
     def matrix_at(i):
-        turn = i % (mats // 2)
-        half_z = n_z // 2
-        target_z = (z - z % 2 + i // (mats // 2) + 2 * middle_out(turn // 2, half_z)) % n_z
-        return (turn % 2) * n_z + target_z
+        batch, turn = i // (mats // BATCHES), i % (mats // BATCHES)
+        side = turn % 2
+        first_z = z - z % BATCHES + (batch + core + 2 * side) % BATCHES
+        return side * n_z + (first_z + BATCHES * middle_out(turn // 2, n_z // BATCHES)) % n_z
 
     def send_one(i, c):
         m = matrix_at(i)

time: 107 us -> 103 us (0.963); the launches traced: 107 us -> 102 us
  Pallas kernels: 101 us -> 95.2 us
    pallas_call x1, Pallas kernels: 101 us -> 95.2 us  [orthogonalized(): pl.pallas_call(partial(kernel, n_dp), out_shape=jax.ShapeDtypeStruct(grad...]
where the time goes in v4:
time: 103 us; the launch traced here: 102 us
  Pallas kernels  95.2 us (92%)
  local copies, waits for them, and re-layouts  4.3 us (4%)
  other arithmetic  1.41 us (1%)
    pallas_call x1, Pallas kernels, orthogonalized(): pl.pallas_call(partial(kernel, n_dp), out_shape=jax.ShapeDtypeStruct(grad...  95.2 us
    unnamed x7, local copies, waits for them, and re-layouts  4.3 us

profile of v4, /device:TPU:6, one launch (start us, length us, event | category | flops | bytes accessed | tf_op | source)
XLA Modules:
  0.0 101.6 jit_solution(12153491511742215292)
XLA Ops:
  0.6 0.0 copy-start.1
  0.6 2.4 %copy.5.mom_ref = f32[32,12,1024]{2,1,0:T(8,128)S(1)} copy(f32[32,12,1024]{2,0,1:T(8,128)} %param.3) | data formatting | bytes 3145728 | tf_op args[1]
  3.1 0.0 copy-done.1
  3.1 0.4 copy.4.grads_ref
  3.5 95.2 %shard_map.41 = bf16[32,12,1024]{2,1,0:T(8,128)(2,1)S(1)} custom-call(bf16[32,12,1024]{2,1,0:T(8,128)(2,1)S(1)} %copy.4.grads_ref, f32[32,12,1024]{2,1,0:T(8,128)S(1)} %copy.5.mom_ref), custom_call_target="tpu_custom_call" | custom-call | flops 4831838208 | bytes 3145728 | tf_op jit(solution)/shard_map/pallas_call | solution.py:308
  98.8 0.0 copy-start
  98.8 1.3 %copy.6 = bf16[32,12,1024]{2,0,1:T(8,128)(2,1)} copy(bf16[32,12,1024]{2,1,0:T(8,128)(2,1)S(1)} %shard_map.41) | data formatting | bytes 1572864
  100.1 0.1 copy-done
  100.2 1.4 %convert_add_fusion = f32[32,12,1024]{2,0,1:T(8,128)} fusion(bf16[32,12,1024]{2,0,1:T(8,128)(2,1)S(1)} %copy-done.1, f32[32,12,1024]{2,0,1:T(8,128)S(1)} %copy-done), kind=kLoop, calls=%fused_computation | loop fusion | flops 1179648 | bytes 3932160 | tf_op jit(solution)/shard_map/add | solution.py:341
Async XLA Ops:
  0.6 2.4 %copy-start.1 = (bf16[32,12,1024]{2,0,1:T(8,128)(2,1)S(1)}, bf16[32,12,1024]{2,0,1:T(8,128)(2,1)}, u32[]{:S(2)}) copy-start(bf16[32,12,1024]{2,0,1:T(8,128)(2,1)} %param.2) | copy-start | bytes 2359300
  98.8 1.4 %copy-start = (f32[32,12,1024]{2,0,1:T(8,128)S(1)}, f32[32,12,1024]{2,0,1:T(8,128)}, u32[]{:S(2)}) copy-start(f32[32,12,1024]{2,0,1:T(8,128)} %param.3) | copy-start | bytes 4718596

commit v5 on v4

--- a/solution.py
+++ b/solution.py
@@ -22,6 +22,7 @@
 TALL = 16
 MAIN = D * ROWS // TALL
 EXTRA = D - MAIN
+LANES = 128
 REST = TALL - ROWS
 SPLITS = ROWS // REST
 SIDES_Y = 4
@@ -29,18 +30,22 @@
 MESH_ID = pl.DeviceIdType.MESH
 
 
-def pack_rows(rows):
-    tail = rows[:, MAIN:]
-    below = jnp.concatenate([tail[REST * j : REST * (j + 1)] for j in range(SPLITS)], axis=1)
-    return jnp.concatenate([rows[:, :MAIN], below], axis=0)
-
-
-def unpack_rows(block):
-    below = block[ROWS:]
-    tail = jnp.concatenate(
-        [below[:, EXTRA * j : EXTRA * (j + 1)] for j in range(SPLITS)], axis=0
-    )
-    return jnp.concatenate([block[:ROWS], tail], axis=1)
+def rows_of(ref, tile, matrix, mats):
+    return ref.at[tile, pl.ds(matrix, ROWS, stride=mats), :]
+
+
+def pack_rows(tiles):
+    for tile in range(MAIN // LANES):
+        part, side = tile // 2, tile % 2
+        below = tiles[MAIN // LANES + side][REST * part : REST * (part + 1)]
+        yield jnp.concatenate([tiles[tile], below], axis=0)
+
+
+def unpack_rows(tiles):
+    for tile in range(MAIN // LANES):
+        yield tiles[tile][:ROWS]
+    for side in range(EXTRA // LANES):
+        yield jnp.concatenate([tiles[2 * part + side][ROWS:] for part in range(SPLITS)], axis=0)
 
 
 def middle_out(i, count):
@@ -74,6 +79,8 @@
     grads_ref,
     mom_ref,
     out_ref,
+    new_mom_ref,
+    rows32,
     sent,
     landed,
     x0,
@@ -128,13 +135,17 @@
 
         lax.fori_loop(0, mats, greet_rest, 0)
 
-    def pack_one(m, c):
-        gradient = grads_ref[m].astype(jnp.float32)
-        momentum = MOMENT * mom_ref[m] + gradient
-        sent[m] = pack_rows(gradient + MOMENT * momentum).astype(jnp.bfloat16)
-        return c
-
-    lax.fori_loop(0, mats, pack_one, 0)
+    def momentum_row(i, c):
+        gradient = grads_ref[i].astype(jnp.float32)
+        momentum = MOMENT * mom_ref[i] + gradient
+        new_mom_ref[i] = momentum
+        nesterov = gradient + MOMENT * momentum
+        here = pl.ds(pl.multiple_of(i * mats, 8), mats)
+        for tile in range(D // LANES):
+            rows32[tile, here, :] = nesterov[:, LANES * tile : LANES * (tile + 1)]
+        return c
+
+    lax.fori_loop(0, ROWS, momentum_row, 0)
 
     @pl.when(owns)
     def _():
@@ -154,6 +165,9 @@
         m = matrix_at(i)
         owner = owner_of(m)
         slot = (dp - owner + n_dp) % n_dp
+        tiles = [rows_of(rows32, tile, m, mats)[...] for tile in range(D // LANES)]
+        for tile, block in enumerate(pack_rows(tiles)):
+            sent[m, :, LANES * tile : LANES * (tile + 1)] = block.astype(jnp.bfloat16)
 
         @pl.when(owner != dp)
         def _():
@@ -277,10 +291,22 @@
     def take_home(i, c):
         m = matrix_at(i)
         pltpu.make_async_copy(home.at[m], home.at[m], home_sem.at[m]).wait()
-        out_ref[m] = unpack_rows(home[m].astype(jnp.float32)).astype(jnp.bfloat16)
+        block = home[m].astype(jnp.float32)
+        tiles = [block[:, LANES * tile : LANES * (tile + 1)] for tile in range(MAIN // LANES)]
+        for tile, rows in enumerate(unpack_rows(tiles)):
+            rows_of(rows32, tile, m, mats)[...] = rows
         return c
 
     lax.fori_loop(0, mats, take_home, 0)
+
+    def update_row(i, c):
+        here = pl.ds(pl.multiple_of(i * mats, 8), mats)
+        for tile in range(D // LANES):
+            columns = slice(LANES * tile, LANES * (tile + 1))
+            out_ref[i, :, columns] = rows32[tile, here, :].astype(jnp.bfloat16)
+        return c
+
+    lax.fori_loop(0, ROWS, update_row, 0)
 
     def sent_done(m, c):
         @pl.when(owner_of(m) != dp)
@@ -307,10 +333,14 @@
     flat = lambda *shape: pltpu.VMEM(shape, jnp.bfloat16)
     return pl.pallas_call(
         partial(kernel, n_dp),
-        out_shape=jax.ShapeDtypeStruct(grads.shape, jnp.bfloat16),
+        out_shape=[
+            jax.ShapeDtypeStruct(grads.shape, jnp.bfloat16),
+            jax.ShapeDtypeStruct(grads.shape, jnp.float32),
+        ],
         in_specs=[pl.BlockSpec(memory_space=pltpu.VMEM)] * 2,
-        out_specs=pl.BlockSpec(memory_space=pltpu.VMEM),
+        out_specs=[pl.BlockSpec(memory_space=pltpu.VMEM)] * 2,
         scratch_shapes=[
+            pltpu.VMEM((D // LANES, ROWS * mats, LANES), jnp.float32),
             packed(mats),
             packed(n_dp),
             flat(height, D),
@@ -337,9 +367,9 @@
 
 def local(grads, momentum):
     n_dp = lax.axis_size("dp")
-    update = orthogonalized(grads, momentum, n_dp)
-    new_momentum = MOMENT * momentum + grads.astype(jnp.float32)
-    return (update, new_momentum)
+    swap = lambda array: jnp.transpose(array, (1, 0, 2))
+    update, new_momentum = orthogonalized(swap(grads), swap(momentum), n_dp)
+    return (swap(update), swap(new_momentum))
 
 
 def solution(mesh):

time: 103 us -> 102 us (level)
  other arithmetic: 1.41 us -> 0 us
    add x1 -> x0, other arithmetic: 1.41 us -> none  [local(): new_momentum = MOMENT * momentum + grads.astype(jnp.float32)]
    unnamed x7 -> x6, local copies, waits for them, and re-layouts: 4.3 us -> 4.56 us
where the time goes in v5:
time: 102 us; the launch traced here: 100 us
  Pallas kernels  95 us (93%)
  local copies, waits for them, and re-layouts  4.56 us (4%)
    pallas_call x1, Pallas kernels, orthogonalized(): pl.pallas_call(partial(kernel, n_dp), out_shape=[jax.ShapeDtypeStruct(gra...  95 us
    unnamed x6, local copies, waits for them, and re-layouts  4.56 us

profile of v5, /device:TPU:6, one launch (start us, length us, event | category | flops | bytes accessed | tf_op | source)
XLA Modules:
  0.0 100.2 jit_solution(14615886511230213751)
XLA Ops:
  0.6 0.0 copy-start
  0.6 1.4 %copy-done = f32[32,12,1024]{2,0,1:T(8,128)S(1)} copy-done((f32[32,12,1024]{2,0,1:T(8,128)S(1)}, f32[32,12,1024]{2,0,1:T(8,128)}, u32[]{:S(2)}) %copy-start) | copy-done | bytes 1572888
  2.0 0.0 copy-start.1
  2.0 1.1 %copy-done.1 = bf16[32,12,1024]{2,0,1:T(8,128)(2,1)S(1)} copy-done((bf16[32,12,1024]{2,0,1:T(8,128)(2,1)S(1)}, bf16[32,12,1024]{2,0,1:T(8,128)(2,1)}, u32[]{:S(2)}) %copy-start.1) | copy-done | bytes 786456
  3.2 95.0 %shard_map.41 = (bf16[12,32,1024]{2,1,0:T(8,128)(2,1)S(1)}, f32[12,32,1024]{2,1,0:T(8,128)S(1)}) custom-call(bf16[12,32,1024]{2,1,0:T(8,128)(2,1)S(1)} %bitcast.7, f32[12,32,1024]{2,1,0:T(8,128)S(1)} %bitcast.6), custom_call_target="tpu_custom_call" | custom-call | flops 4831838208 | bytes 3145728 | tf_op jit(solution)/shard_map/pallas_call | solution.py:334
  98.2 0.9 copy.6
  99.1 1.1 %copy.7 = f32[32,12,1024]{2,0,1:T(8,128)} copy(f32[32,12,1024]{2,0,1:T(8,128)S(1)} %bitcast.4) | data formatting | bytes 3145728
Async XLA Ops:
  0.6 1.4 %copy-start = (f32[32,12,1024]{2,0,1:T(8,128)S(1)}, f32[32,12,1024]{2,0,1:T(8,128)}, u32[]{:S(2)}) copy-start(f32[32,12,1024]{2,0,1:T(8,128)} %param.3) | copy-start | bytes 4718596
  2.0 1.1 %copy-start.1 = (bf16[32,12,1024]{2,0,1:T(8,128)(2,1)S(1)}, bf16[32,12,1024]{2,0,1:T(8,128)(2,1)}, u32[]{:S(2)}) copy-start(bf16[32,12,1024]{2,0,1:T(8,128)(2,1)} %param.2) | copy-start | bytes 2359300

commit v6 on v5

--- a/solution.py
+++ b/solution.py
@@ -27,6 +27,7 @@
 SPLITS = ROWS // REST
 SIDES_Y = 4
 BATCHES = 4
+EARLY = 3
 MESH_ID = pl.DeviceIdType.MESH
 
 
@@ -91,10 +92,16 @@
     home,
     sel,
     sel_t,
+    via,
+    back,
     sent_sem,
     landed_sem,
     away_sem,
     home_sem,
+    via_sem,
+    via_sent_sem,
+    back_sem,
+    back_sent_sem,
 ):
     n_z = n_dp // SIDES_Y
     mats = n_dp // 2
@@ -109,6 +116,20 @@
     y, z = dp // n_z, dp % n_z
     owns = y % 2 == core
     mine = (y // 2) * n_z + z
+    quarter = n_z // 4
+
+    def along_z(rises):
+        return (z + jnp.where(rises, quarter, n_z - quarter)) % n_z
+
+    def copy_to(target, src, dst, send_sem, recv_sem):
+        return pltpu.make_async_remote_copy(
+            src_ref=src,
+            dst_ref=dst,
+            send_sem=send_sem,
+            recv_sem=recv_sem,
+            device_id=(target, expert),
+            device_id_type=MESH_ID,
+        )
 
     def owner_of(matrix):
         return (core + 2 * (matrix // n_z)) * n_z + matrix % n_z
@@ -134,6 +155,12 @@
             return c
 
         lax.fori_loop(0, mats, greet_rest, 0)
+
+    @pl.when(jnp.logical_not(owns))
+    def _():
+        for rises in (True, False):
+            other = y * n_z + along_z(rises)
+            pl.semaphore_signal(barrier, inc=1, device_id=(other, expert), device_id_type=MESH_ID)
 
     def momentum_row(i, c):
         gradient = grads_ref[i].astype(jnp.float32)
@@ -153,7 +180,7 @@
 
     @pl.when(jnp.logical_not(owns))
     def _():
-        pl.semaphore_wait(barrier, mats)
+        pl.semaphore_wait(barrier, mats + 2)
 
     def matrix_at(i):
         batch, turn = i // (mats // BATCHES), i % (mats // BATCHES)
@@ -161,32 +188,60 @@
         first_z = z - z % BATCHES + (batch + core + 2 * side) % BATCHES
         return side * n_z + (first_z + BATCHES * middle_out(turn // 2, n_z // BATCHES)) % n_z
 
+    def pack_one(m):
+        tiles = [rows_of(rows32, tile, m, mats)[...] for tile in range(D // LANES)]
+        for tile, block in enumerate(pack_rows(tiles)):
+            sent[m, :, LANES * tile : LANES * (tile + 1)] = block.astype(jnp.bfloat16)
+
+    def send_far(turn, c):
+        m = turn * n_z + (z + n_z // 2) % n_z
+        relay = (core + 2 * turn) * n_z + along_z((z // 2 + turn) % 2 == 0)
+        pack_one(m)
+        copy_to(relay, sent.at[m], via.at[y], sent_sem.at[m], via_sem.at[y]).start()
+        return c
+
+    lax.fori_loop(0, 2, send_far, 0)
+
     def send_one(i, c):
         m = matrix_at(i)
         owner = owner_of(m)
         slot = (dp - owner + n_dp) % n_dp
-        tiles = [rows_of(rows32, tile, m, mats)[...] for tile in range(D // LANES)]
-        for tile, block in enumerate(pack_rows(tiles)):
-            sent[m, :, LANES * tile : LANES * (tile + 1)] = block.astype(jnp.bfloat16)
-
-        @pl.when(owner != dp)
+        far = m % n_z == (z + n_z // 2) % n_z
+
+        @pl.when((owner != dp) & jnp.logical_not(far))
         def _():
-            pltpu.make_async_remote_copy(
-                src_ref=sent.at[m],
-                dst_ref=landed.at[slot],
-                send_sem=sent_sem.at[m],
-                recv_sem=landed_sem.at[slot],
-                device_id=(owner, expert),
-                device_id_type=MESH_ID,
+            pack_one(m)
+            copy_to(
+                owner, sent.at[m], landed.at[slot], sent_sem.at[m], landed_sem.at[slot]
             ).start()
 
         @pl.when(owner == dp)
         def _():
+            pack_one(m)
             pltpu.make_async_copy(sent.at[m], landed.at[0], landed_sem.at[0]).start()
 
         return c
 
-    lax.fori_loop(0, mats, send_one, 0)
+    lax.fori_loop(0, EARLY, send_one, 0)
+
+    @pl.when(owns)
+    def _():
+        rises = ((z + n_z - quarter) // 2 + y // 2) % 2 == 0
+        source_z = along_z(jnp.logical_not(rises))
+        owner = y * n_z + along_z(rises)
+
+        def pass_on(source_y, c):
+            slot = (source_y * n_z + source_z - owner + n_dp) % n_dp
+            block = via.at[source_y]
+            pltpu.make_async_copy(block, block, via_sem.at[source_y]).wait()
+            copy_to(
+                owner, block, landed.at[slot], via_sent_sem.at[source_y], landed_sem.at[slot]
+            ).start()
+            return c
+
+        lax.fori_loop(0, SIDES_Y, pass_on, 0)
+
+    lax.fori_loop(EARLY, mats, send_one, 0)
 
     @pl.when(owns)
     def _():
@@ -265,16 +320,27 @@
             def return_one(t, c):
                 slot = g * group + middle_out(t, group)
                 target = (dp + slot) % n_dp
-
-                @pl.when(slot != 0)
+                target_y = target // n_z
+                far = slot % n_z == n_z // 2
+
+                @pl.when((slot != 0) & jnp.logical_not(far))
                 def _():
-                    pltpu.make_async_remote_copy(
-                        src_ref=away.at[slot],
-                        dst_ref=home.at[mine],
-                        send_sem=away_sem.at[slot],
-                        recv_sem=home_sem.at[mine],
-                        device_id=(target, expert),
-                        device_id_type=MESH_ID,
+                    copy_to(
+                        target, away.at[slot], home.at[mine], away_sem.at[slot], home_sem.at[mine]
+                    ).start()
+
+                @pl.when(far)
+                def _():
+                    shift = (target_y + 1 + core) % 2
+                    relay_y = (target_y + shift) % SIDES_Y
+                    relay = relay_y * n_z + along_z((z // 2 + target_y) % 2 == 0)
+                    place = 2 * (y // 2) + shift
+                    copy_to(
+                        relay,
+                        away.at[slot],
+                        back.at[place],
+                        away_sem.at[slot],
+                        back_sem.at[place],
                     ).start()
 
                 @pl.when(slot == 0)
@@ -287,6 +353,24 @@
             return c
 
         lax.fori_loop(0, n_dp // group, finish_group, 0)
+
+    @pl.when(jnp.logical_not(owns))
+    def _():
+        flip = ((z + 2 * SIDES_Y - core) % SIDES_Y) // 2
+
+        def pass_back(i, c):
+            half, shift = (i // 2 + flip) % 2, i % 2
+            target_y = (y + SIDES_Y - shift) % SIDES_Y
+            rises = ((z + n_z - quarter) // 2 + target_y) % 2 == 0
+            m = half * n_z + along_z(jnp.logical_not(rises))
+            target = target_y * n_z + along_z(rises)
+            place = 2 * half + shift
+            block = back.at[place]
+            pltpu.make_async_copy(block, block, back_sem.at[place]).wait()
+            copy_to(target, block, home.at[m], back_sent_sem.at[place], home_sem.at[m]).start()
+            return c
+
+        lax.fori_loop(0, SIDES_Y, pass_back, 0)
 
     def take_home(i, c):
         m = matrix_at(i)
@@ -324,6 +408,20 @@
             return c
 
         lax.fori_loop(1, n_dp, away_done, 0)
+
+        def passed_on(side, c):
+            pltpu.make_async_copy(via.at[side], via.at[side], via_sent_sem.at[side]).wait()
+            return c
+
+        lax.fori_loop(0, SIDES_Y, passed_on, 0)
+
+    @pl.when(jnp.logical_not(owns))
+    def _():
+        def passed_back(side, c):
+            pltpu.make_async_copy(back.at[side], back.at[side], back_sent_sem.at[side]).wait()
+            return c
+
+        lax.fori_loop(0, SIDES_Y, passed_back, 0)
 
 
 def orthogonalized(grads, momentum, n_dp):
@@ -351,10 +449,13 @@
             packed(mats),
             flat(SPLITS + 1, ROWS * group, TALL * group),
             flat(SPLITS + 1, TALL * group, ROWS * group),
+            packed(SIDES_Y),
+            packed(SIDES_Y),
             pltpu.SemaphoreType.DMA((mats,)),
             pltpu.SemaphoreType.DMA((n_dp,)),
             pltpu.SemaphoreType.DMA((n_dp,)),
             pltpu.SemaphoreType.DMA((mats,)),
+            *[pltpu.SemaphoreType.DMA((SIDES_Y,))] * 4,
         ],
         compiler_params=pltpu.CompilerParams(
             collective_id=0, has_side_effects=True, vmem_limit_bytes=40 * 1024 * 1024

time: 102 us -> 109 us (1.069); the launches traced: 100 us -> 109 us
  Pallas kernels: 95 us -> 104 us
    pallas_call x1, Pallas kernels: 95 us -> 104 us  [orthogonalized(): pl.pallas_call(partial(kernel, n_dp), out_shape=[jax.ShapeDtypeStruct(gra...]
where the time goes in v6:
time: 109 us
  Pallas kernels  104 us (95%)
  local copies, waits for them, and re-layouts  4.56 us (4%)
    pallas_call x1, Pallas kernels, orthogonalized(): pl.pallas_call(partial(kernel, n_dp), out_shape=[jax.ShapeDtypeStruct(gra...  104 us
    unnamed x6, local copies, waits for them, and re-layouts  4.56 us

profile of v6, /device:TPU:6, one launch (start us, length us, event | category | flops | bytes accessed | tf_op | source)
XLA Modules:
  0.0 109.1 jit_solution(10024502729604962517)
XLA Ops:
  0.6 0.0 copy-start
  0.6 1.4 %copy-done = f32[32,12,1024]{2,0,1:T(8,128)S(1)} copy-done((f32[32,12,1024]{2,0,1:T(8,128)S(1)}, f32[32,12,1024]{2,0,1:T(8,128)}, u32[]{:S(2)}) %copy-start) | copy-done | bytes 1572888
  2.0 0.0 copy-start.1
  2.0 1.1 %copy-done.1 = bf16[32,12,1024]{2,0,1:T(8,128)(2,1)S(1)} copy-done((bf16[32,12,1024]{2,0,1:T(8,128)(2,1)S(1)}, bf16[32,12,1024]{2,0,1:T(8,128)(2,1)}, u32[]{:S(2)}) %copy-start.1) | copy-done | bytes 786456
  3.2 103.9 %shard_map.41 = (bf16[12,32,1024]{2,1,0:T(8,128)(2,1)S(1)}, f32[12,32,1024]{2,1,0:T(8,128)S(1)}) custom-call(bf16[12,32,1024]{2,1,0:T(8,128)(2,1)S(1)} %bitcast.7, f32[12,32,1024]{2,1,0:T(8,128)S(1)} %bitcast.6), custom_call_target="tpu_custom_call" | custom-call | flops 4831838208 | bytes 3145728 | tf_op jit(solution)/shard_map/pallas_call | solution.py:432
  107.0 0.9 copy.6
  107.9 1.1 %copy.7 = f32[32,12,1024]{2,0,1:T(8,128)} copy(f32[32,12,1024]{2,0,1:T(8,128)S(1)} %bitcast.4) | data formatting | bytes 3145728
Async XLA Ops:
  0.6 1.4 %copy-start = (f32[32,12,1024]{2,0,1:T(8,128)S(1)}, f32[32,12,1024]{2,0,1:T(8,128)}, u32[]{:S(2)}) copy-start(f32[32,12,1024]{2,0,1:T(8,128)} %param.3) | copy-start | bytes 4718596
  2.0 1.1 %copy-start.1 = (bf16[32,12,1024]{2,0,1:T(8,128)(2,1)S(1)}, bf16[32,12,1024]{2,0,1:T(8,128)(2,1)}, u32[]{:S(2)}) copy-start(bf16[32,12,1024]{2,0,1:T(8,128)(2,1)} %param.2) | copy-start | bytes 2359300

commit v7 on v5

--- a/solution.py
+++ b/solution.py
@@ -27,6 +27,7 @@
 SPLITS = ROWS // REST
 SIDES_Y = 4
 BATCHES = 4
+VMEM_MIB = 62
 MESH_ID = pl.DeviceIdType.MESH
 
 
@@ -76,10 +77,12 @@
 
 def kernel(
     n_dp,
+    grads_hbm,
+    mom_hbm,
+    out_ref,
+    new_mom_hbm,
     grads_ref,
     mom_ref,
-    out_ref,
-    new_mom_ref,
     rows32,
     sent,
     landed,
@@ -95,13 +98,15 @@
     landed_sem,
     away_sem,
     home_sem,
+    read_sem,
+    write_sem,
 ):
     n_z = n_dp // SIDES_Y
     mats = n_dp // 2
     height = ROWS * n_dp
     group = min(16, n_dp)
     plain_rows, packed_rows = ROWS * group, TALL * group
-    block_rows = 256 if height % 256 == 0 else plain_rows
+    block = 256 if height % 256 == 0 else 128
 
     dp = lax.axis_index("dp")
     expert = lax.axis_index("expert")
@@ -113,6 +118,20 @@
     def owner_of(matrix):
         return (core + 2 * (matrix // n_z)) * n_z + matrix % n_z
 
+    def read(i):
+        yield pltpu.make_async_copy(mom_hbm.at[i], mom_ref.at[i], read_sem.at[0, i])
+        yield pltpu.make_async_copy(grads_hbm.at[i], grads_ref.at[i], read_sem.at[1, i])
+
+    def write(i):
+        return pltpu.make_async_copy(mom_ref.at[i], new_mom_hbm.at[i], write_sem.at[i])
+
+    def start_read(i, c):
+        for copy in read(i):
+            copy.start()
+        return c
+
+    lax.fori_loop(0, ROWS, start_read, 0)
+
     barrier = pltpu.get_barrier_semaphore()
 
     def greet_owner(i, c):
@@ -136,9 +155,12 @@
         lax.fori_loop(0, mats, greet_rest, 0)
 
     def momentum_row(i, c):
+        for copy in read(i):
+            copy.wait()
         gradient = grads_ref[i].astype(jnp.float32)
         momentum = MOMENT * mom_ref[i] + gradient
-        new_mom_ref[i] = momentum
+        mom_ref[i] = momentum
+        write(i).start()
         nesterov = gradient + MOMENT * momentum
         here = pl.ds(pl.multiple_of(i * mats, 8), mats)
         for tile in range(D // LANES):
@@ -157,9 +179,10 @@
 
     def matrix_at(i):
         batch, turn = i // (mats // BATCHES), i % (mats // BATCHES)
-        side = turn % 2
+        each = n_z // BATCHES
+        side = (turn // each + (y + SIDES_Y - core) % SIDES_Y // 2) % 2
         first_z = z - z % BATCHES + (batch + core + 2 * side) % BATCHES
-        return side * n_z + (first_z + BATCHES * middle_out(turn // 2, n_z // BATCHES)) % n_z
+        return side * n_z + (first_z + BATCHES * middle_out(turn % each, each)) % n_z
 
     def send_one(i, c):
         m = matrix_at(i)
@@ -195,58 +218,65 @@
             sel[part] = selector(0, 1, (plain_rows, packed_rows), which)
             sel_t[part] = selector(1, 0, (packed_rows, plain_rows), which)
 
-        def squares(slot, total):
-            pltpu.make_async_copy(landed.at[slot], landed.at[slot], landed_sem.at[slot]).wait()
-            values = landed[slot].astype(jnp.float32)
-            return total + values * values
-
-        total = lax.fori_loop(0, n_dp, squares, jnp.zeros((TALL, MAIN), jnp.float32))
+        def unpack_group(g, total):
+            def squares(t, total):
+                slot = g * group + t
+                block = landed.at[slot]
+                pltpu.make_async_copy(block, block, landed_sem.at[slot]).wait()
+                values = block[...].astype(jnp.float32)
+                return total + values * values
+
+            total = lax.fori_loop(0, group, squares, total)
+            block = landed[pl.ds(pl.multiple_of(g * group, group), group)]
+            block = block.reshape(packed_rows, MAIN)
+            rows = pl.ds(pl.multiple_of(g * plain_rows, 16), plain_rows)
+            x0[rows, :MAIN] = dot(sel[0], block).astype(jnp.bfloat16)
+            tail = dot(sel[1], block[:, :EXTRA])
+            for part in range(1, SPLITS):
+                tail = tail + dot(sel[part + 1], block[:, EXTRA * part : EXTRA * (part + 1)])
+            x0[rows, MAIN:] = tail.astype(jnp.bfloat16)
+            return total
+
+        total = jnp.zeros((TALL, MAIN), jnp.float32)
+        total = lax.fori_loop(0, n_dp // group, unpack_group, total)
         norm = jnp.sqrt(jnp.sum(total, axis=(0, 1), keepdims=True)) + EPS
-
-        def unpack_group(g, c):
-            block = landed[pl.ds(pl.multiple_of(g * group, group), group)]
-            block = block.reshape(packed_rows, MAIN).astype(jnp.float32)
-            start = (block / norm).astype(jnp.bfloat16)
-            rows = pl.ds(pl.multiple_of(g * plain_rows, 16), plain_rows)
-            x0[rows, :MAIN] = dot(sel[0], start).astype(jnp.bfloat16)
-            tail = dot(sel[1], start[:, :EXTRA])
-            for part in range(1, SPLITS):
-                tail = tail + dot(sel[part + 1], start[:, EXTRA * part : EXTRA * (part + 1)])
-            x0[rows, MAIN:] = tail.astype(jnp.bfloat16)
+        scale_in = 1.0 / norm
+
+        def start_rows(r, c):
+            rows = pl.ds(pl.multiple_of(r * plain_rows, 16), plain_rows)
+            x0[rows] = (x0[rows].astype(jnp.float32) * scale_in).astype(jnp.bfloat16)
             return c
 
-        lax.fori_loop(0, n_dp // group, unpack_group, 0)
+        lax.fori_loop(0, n_dp // group, start_rows, 0)
 
         state = x0
         for step in range(ITERS):
 
-            def gram_rows(r, c, state=state):
-                rows = pl.ds(pl.multiple_of(r * block_rows, 16), block_rows)
-                gram[rows] = dot_t(state[rows], state[...]).astype(jnp.bfloat16)
+            def gram_columns(r, c, state=state):
+                part = pl.ds(pl.multiple_of(r * block, 128), block)
+                gram[:, part] = dot_t(state[...], state[part]).astype(jnp.bfloat16)
                 return c
 
-            def mixer_rows(r, c):
-                rows = pl.ds(pl.multiple_of(r * block_rows, 16), block_rows)
-                some = gram[rows]
-                square = dot(some, gram[...])
-                mixed = B_COEF * some.astype(jnp.float32) + C_COEF * square
-                mixer[rows] = mixed.astype(jnp.bfloat16)
+            def mixer_columns(r, c):
+                part = pl.ds(pl.multiple_of(r * block, 128), block)
+                some = gram[:, part]
+                mixed = B_COEF * some.astype(jnp.float32) + C_COEF * dot(gram[...], some)
+                mixer[:, part] = mixed.astype(jnp.bfloat16)
                 return c
 
-            lax.fori_loop(0, height // block_rows, gram_rows, 0)
-            lax.fori_loop(0, height // block_rows, mixer_rows, 0)
+            lax.fori_loop(0, height // block, gram_columns, 0)
+            lax.fori_loop(0, height // block, mixer_columns, 0)
 
             if step < ITERS - 1:
 
-                def next_rows(r, c, state=state):
-                    rows = pl.ds(pl.multiple_of(r * block_rows, 16), block_rows)
-                    moved = dot(mixer[rows], state[...])
-                    x1[rows] = (A_COEF * state[rows].astype(jnp.float32) + moved).astype(
-                        jnp.bfloat16
-                    )
+                def next_columns(r, c, state=state):
+                    part = pl.ds(pl.multiple_of(r * block, 128), block)
+                    some = state[:, part]
+                    moved = dot(mixer[...], some)
+                    x1[:, part] = (A_COEF * some.astype(jnp.float32) + moved).astype(jnp.bfloat16)
                     return c
 
-                lax.fori_loop(0, height // block_rows, next_rows, 0)
+                lax.fori_loop(0, D // block, next_columns, 0)
                 state = x1
 
         scale = 0.2 * math.sqrt(max(H, D))
@@ -300,6 +330,7 @@
     lax.fori_loop(0, mats, take_home, 0)
 
     def update_row(i, c):
+        write(i).wait()
         here = pl.ds(pl.multiple_of(i * mats, 8), mats)
         for tile in range(D // LANES):
             columns = slice(LANES * tile, LANES * (tile + 1))
@@ -337,9 +368,14 @@
             jax.ShapeDtypeStruct(grads.shape, jnp.bfloat16),
             jax.ShapeDtypeStruct(grads.shape, jnp.float32),
         ],
-        in_specs=[pl.BlockSpec(memory_space=pltpu.VMEM)] * 2,
-        out_specs=[pl.BlockSpec(memory_space=pltpu.VMEM)] * 2,
+        in_specs=[pl.BlockSpec(memory_space=pltpu.HBM)] * 2,
+        out_specs=[
+            pl.BlockSpec(memory_space=pltpu.VMEM),
+            pl.BlockSpec(memory_space=pltpu.HBM),
+        ],
         scratch_shapes=[
+            pltpu.VMEM(grads.shape, jnp.bfloat16),
+            pltpu.VMEM(grads.shape, jnp.float32),
             pltpu.VMEM((D // LANES, ROWS * mats, LANES), jnp.float32),
             packed(mats),
             packed(n_dp),
@@ -355,9 +391,11 @@
             pltpu.SemaphoreType.DMA((n_dp,)),
             pltpu.SemaphoreType.DMA((n_dp,)),
             pltpu.SemaphoreType.DMA((mats,)),
+            pltpu.SemaphoreType.DMA((2, ROWS)),
+            pltpu.SemaphoreType.DMA((ROWS,)),
         ],
         compiler_params=pltpu.CompilerParams(
-            collective_id=0, has_side_effects=True, vmem_limit_bytes=40 * 1024 * 1024
+            collective_id=0, has_side_effects=True, vmem_limit_bytes=VMEM_MIB * 1024 * 1024
         ),
         cost_estimate=pl.CostEstimate(
             flops=8 * height * height * D, bytes_accessed=8 * grads.size, transcendentals=0

time: 102 us -> 103 us (level); the launches traced: 100 us -> 103 us
  Pallas kernels: 95 us -> 99.3 us
  local copies, waits for them, and re-layouts: 4.56 us -> 3.33 us
    pallas_call x1, Pallas kernels: 95 us -> 99.3 us  [orthogonalized(): pl.pallas_call(partial(kernel, n_dp), out_shape=[jax.ShapeDtypeStruct(gra...]
    unnamed x6 -> x4, local copies, waits for them, and re-layouts: 4.56 us -> 3.33 us
where the time goes in v7:
time: 103 us
  Pallas kernels  99.3 us (96%)
  local copies, waits for them, and re-layouts  3.33 us (3%)
    pallas_call x1, Pallas kernels, orthogonalized(): pl.pallas_call(partial(kernel, n_dp), out_shape=[jax.ShapeDtypeStruct(gra...  99.3 us
    unnamed x4, local copies, waits for them, and re-layouts  3.33 us

profile of v7, /device:TPU:6, one launch (start us, length us, event | category | flops | bytes accessed | tf_op | source)
XLA Modules:
  0.0 103.3 jit_solution(11418890202237178855)
XLA Ops:
  0.6 99.3 %shard_map.41 = (bf16[12,32,1024]{2,1,0:T(8,128)(2,1)}, f32[12,32,1024]{2,1,0:T(8,128)}) custom-call(bf16[12,32,1024]{2,1,0:T(8,128)(2,1)} %bitcast.7, f32[12,32,1024]{2,1,0:T(8,128)} %bitcast.6), custom_call_target="tpu_custom_call" | custom-call | flops 4831838208 | bytes 3145728 | tf_op jit(solution)/shard_map/pallas_call | solution.py:365
  100.0 0.0 copy-start
  100.0 2.2 %copy.6 = bf16[32,12,1024]{2,0,1:T(8,128)(2,1)} copy(bf16[32,12,1024]{2,0,1:T(8,128)(2,1)} %bitcast.5) | data formatting | bytes 1572864
  102.1 0.0 copy-done
  102.2 1.1 %copy.7 = f32[32,12,1024]{2,0,1:T(8,128)} copy(f32[32,12,1024]{2,0,1:T(8,128)S(1)} %bitcast.4) | data formatting | bytes 3145728
Async XLA Ops:
  100.0 2.2 %copy-start = (f32[12,32,1024]{2,1,0:T(8,128)S(1)}, f32[12,32,1024]{2,1,0:T(8,128)}, u32[]{:S(2)}) copy-start(f32[12,32,1024]{2,1,0:T(8,128)} %get-tuple-element.5) | copy-start | bytes 4718596

commit v8 on v7

--- a/solution.py
+++ b/solution.py
@@ -26,8 +26,7 @@
 REST = TALL - ROWS
 SPLITS = ROWS // REST
 SIDES_Y = 4
-BATCHES = 4
-VMEM_MIB = 62
+BATCHES = 2
 MESH_ID = pl.DeviceIdType.MESH
 
 
@@ -77,12 +76,10 @@
 
 def kernel(
     n_dp,
-    grads_hbm,
-    mom_hbm,
-    out_ref,
-    new_mom_hbm,
     grads_ref,
     mom_ref,
+    out_ref,
+    new_mom_ref,
     rows32,
     sent,
     landed,
@@ -98,8 +95,6 @@
     landed_sem,
     away_sem,
     home_sem,
-    read_sem,
-    write_sem,
 ):
     n_z = n_dp // SIDES_Y
     mats = n_dp // 2
@@ -108,6 +103,20 @@
     plain_rows, packed_rows = ROWS * group, TALL * group
     block = 256 if height % 256 == 0 else 128
 
+    def send_to(target, src, dst, send_sem, recv_sem):
+        copy = pltpu.make_async_remote_copy(
+            src_ref=src,
+            dst_ref=dst,
+            send_sem=send_sem,
+            recv_sem=recv_sem,
+            device_id=(target, expert),
+            device_id_type=MESH_ID,
+        )
+
+        @pl.when(target != dp)
+        def _():
+            copy.start()
+
     dp = lax.axis_index("dp")
     expert = lax.axis_index("expert")
     core = expert % 2
@@ -118,20 +127,6 @@
     def owner_of(matrix):
         return (core + 2 * (matrix // n_z)) * n_z + matrix % n_z
 
-    def read(i):
-        yield pltpu.make_async_copy(mom_hbm.at[i], mom_ref.at[i], read_sem.at[0, i])
-        yield pltpu.make_async_copy(grads_hbm.at[i], grads_ref.at[i], read_sem.at[1, i])
-
-    def write(i):
-        return pltpu.make_async_copy(mom_ref.at[i], new_mom_hbm.at[i], write_sem.at[i])
-
-    def start_read(i, c):
-        for copy in read(i):
-            copy.start()
-        return c
-
-    lax.fori_loop(0, ROWS, start_read, 0)
-
     barrier = pltpu.get_barrier_semaphore()
 
     def greet_owner(i, c):
@@ -155,12 +150,9 @@
         lax.fori_loop(0, mats, greet_rest, 0)
 
     def momentum_row(i, c):
-        for copy in read(i):
-            copy.wait()
         gradient = grads_ref[i].astype(jnp.float32)
         momentum = MOMENT * mom_ref[i] + gradient
-        mom_ref[i] = momentum
-        write(i).start()
+        new_mom_ref[i] = momentum
         nesterov = gradient + MOMENT * momentum
         here = pl.ds(pl.multiple_of(i * mats, 8), mats)
         for tile in range(D // LANES):
@@ -179,10 +171,9 @@
 
     def matrix_at(i):
         batch, turn = i // (mats // BATCHES), i % (mats // BATCHES)
-        each = n_z // BATCHES
-        side = (turn // each + (y + SIDES_Y - core) % SIDES_Y // 2) % 2
-        first_z = z - z % BATCHES + (batch + core + 2 * side) % BATCHES
-        return side * n_z + (first_z + BATCHES * middle_out(turn % each, each)) % n_z
+        side = turn % 2
+        first_z = z - z % BATCHES + (batch + core) % BATCHES
+        return side * n_z + (first_z + BATCHES * middle_out(turn // 2, n_z // BATCHES)) % n_z
 
     def send_one(i, c):
         m = matrix_at(i)
@@ -192,16 +183,7 @@
         for tile, block in enumerate(pack_rows(tiles)):
             sent[m, :, LANES * tile : LANES * (tile + 1)] = block.astype(jnp.bfloat16)
 
-        @pl.when(owner != dp)
-        def _():
-            pltpu.make_async_remote_copy(
-                src_ref=sent.at[m],
-                dst_ref=landed.at[slot],
-                send_sem=sent_sem.at[m],
-                recv_sem=landed_sem.at[slot],
-                device_id=(owner, expert),
-                device_id_type=MESH_ID,
-            ).start()
+        send_to(owner, sent.at[m], landed.at[slot], sent_sem.at[m], landed_sem.at[slot])
 
         @pl.when(owner == dp)
         def _():
@@ -296,16 +278,9 @@
                 slot = g * group + middle_out(t, group)
                 target = (dp + slot) % n_dp
 
-                @pl.when(slot != 0)
-                def _():
-                    pltpu.make_async_remote_copy(
-                        src_ref=away.at[slot],
-                        dst_ref=home.at[mine],
-                        send_sem=away_sem.at[slot],
-                        recv_sem=home_sem.at[mine],
-                        device_id=(target, expert),
-                        device_id_type=MESH_ID,
-                    ).start()
+                send_to(
+                    target, away.at[slot], home.at[mine], away_sem.at[slot], home_sem.at[mine]
+                )
 
                 @pl.when(slot == 0)
                 def _():
@@ -330,7 +305,6 @@
     lax.fori_loop(0, mats, take_home, 0)
 
     def update_row(i, c):
-        write(i).wait()
         here = pl.ds(pl.multiple_of(i * mats, 8), mats)
         for tile in range(D // LANES):
             columns = slice(LANES * tile, LANES * (tile + 1))
@@ -368,14 +342,9 @@
             jax.ShapeDtypeStruct(grads.shape, jnp.bfloat16),
             jax.ShapeDtypeStruct(grads.shape, jnp.float32),
         ],
-        in_specs=[pl.BlockSpec(memory_space=pltpu.HBM)] * 2,
-        out_specs=[
-            pl.BlockSpec(memory_space=pltpu.VMEM),
-            pl.BlockSpec(memory_space=pltpu.HBM),
-        ],
+        in_specs=[pl.BlockSpec(memory_space=pltpu.VMEM)] * 2,
+        out_specs=[pl.BlockSpec(memory_space=pltpu.VMEM)] * 2,
         scratch_shapes=[
-            pltpu.VMEM(grads.shape, jnp.bfloat16),
-            pltpu.VMEM(grads.shape, jnp.float32),
             pltpu.VMEM((D // LANES, ROWS * mats, LANES), jnp.float32),
             packed(mats),
             packed(n_dp),
@@ -391,11 +360,9 @@
             pltpu.SemaphoreType.DMA((n_dp,)),
             pltpu.SemaphoreType.DMA((n_dp,)),
             pltpu.SemaphoreType.DMA((mats,)),
-            pltpu.SemaphoreType.DMA((2, ROWS)),
-            pltpu.SemaphoreType.DMA((ROWS,)),
         ],
         compiler_params=pltpu.CompilerParams(
-            collective_id=0, has_side_effects=True, vmem_limit_bytes=VMEM_MIB * 1024 * 1024
+            collective_id=0, has_side_effects=True, vmem_limit_bytes=40 * 1024 * 1024
         ),
         cost_estimate=pl.CostEstimate(
             flops=8 * height * height * D, bytes_accessed=8 * grads.size, transcendentals=0

time: 103 us -> 107 us (1.039)
  the two profiles are of different devices: /device:TPU:6 before, /device:TPU:22 now
where the time goes in v8:
time: 107 us; the launch traced here: 106 us
  Pallas kernels  101 us (94%)
  local copies, waits for them, and re-layouts  4.56 us (4%)
    pallas_call x1, Pallas kernels, orthogonalized(): pl.pallas_call(partial(kernel, n_dp), out_shape=[jax.ShapeDtypeStruct(gra...  101 us
    unnamed x6, local copies, waits for them, and re-layouts  4.56 us

profile of v8, /device:TPU:22, one launch (start us, length us, event | category | flops | bytes accessed | tf_op | source)
XLA Modules:
  0.0 106.4 jit_solution(14803909401832924026)
XLA Ops:
  0.6 0.0 copy-start
  0.6 1.4 %copy-done = f32[32,12,1024]{2,0,1:T(8,128)S(1)} copy-done((f32[32,12,1024]{2,0,1:T(8,128)S(1)}, f32[32,12,1024]{2,0,1:T(8,128)}, u32[]{:S(2)}) %copy-start) | copy-done | bytes 1572888
  2.0 0.0 copy-start.1
  2.0 1.1 %copy-done.1 = bf16[32,12,1024]{2,0,1:T(8,128)(2,1)S(1)} copy-done((bf16[32,12,1024]{2,0,1:T(8,128)(2,1)S(1)}, bf16[32,12,1024]{2,0,1:T(8,128)(2,1)}, u32[]{:S(2)}) %copy-start.1) | copy-done | bytes 786456
  3.2 101.2 %shard_map.41 = (bf16[12,32,1024]{2,1,0:T(8,128)(2,1)S(1)}, f32[12,32,1024]{2,1,0:T(8,128)S(1)}) custom-call(bf16[12,32,1024]{2,1,0:T(8,128)(2,1)S(1)} %bitcast.7, f32[12,32,1024]{2,1,0:T(8,128)S(1)} %bitcast.6), custom_call_target="tpu_custom_call" | custom-call | flops 4831838208 | bytes 3145728 | tf_op jit(solution)/shard_map/pallas_call | solution.py:339
  104.4 0.9 copy.6
  105.3 1.1 %copy.7 = f32[32,12,1024]{2,0,1:T(8,128)} copy(f32[32,12,1024]{2,0,1:T(8,128)S(1)} %bitcast.4) | data formatting | bytes 3145728
Async XLA Ops:
  0.6 1.4 %copy-start = (f32[32,12,1024]{2,0,1:T(8,128)S(1)}, f32[32,12,1024]{2,0,1:T(8,128)}, u32[]{:S(2)}) copy-start(f32[32,12,1024]{2,0,1:T(8,128)} %param.3) | copy-start | bytes 4718596
  2.0 1.1 %copy-start.1 = (bf16[32,12,1024]{2,0,1:T(8,128)(2,1)S(1)}, bf16[32,12,1024]{2,0,1:T(8,128)(2,1)}, u32[]{:S(2)}) copy-start(bf16[32,12,1024]{2,0,1:T(8,128)(2,1)} %param.2) | copy-start | bytes 2359300

commit v9 on v8

--- a/solution.py
+++ b/solution.py
@@ -26,7 +26,7 @@
 REST = TALL - ROWS
 SPLITS = ROWS // REST
 SIDES_Y = 4
-BATCHES = 2
+BATCHES = 4
 MESH_ID = pl.DeviceIdType.MESH
 
 
@@ -172,7 +172,7 @@
     def matrix_at(i):
         batch, turn = i // (mats // BATCHES), i % (mats // BATCHES)
         side = turn % 2
-        first_z = z - z % BATCHES + (batch + core) % BATCHES
+        first_z = z - z % BATCHES + (batch + core + 2 * side) % BATCHES
         return side * n_z + (first_z + BATCHES * middle_out(turn // 2, n_z // BATCHES)) % n_z
 
     def send_one(i, c):

time: 107 us -> 102 us (0.953)
  the two profiles are of different devices: /device:TPU:22 before, /device:TPU:6 now
where the time goes in v9:
time: 102 us; the launch traced here: 100 us
  Pallas kernels  95.1 us (93%)
  local copies, waits for them, and re-layouts  4.56 us (4%)
    pallas_call x1, Pallas kernels, orthogonalized(): pl.pallas_call(partial(kernel, n_dp), out_shape=[jax.ShapeDtypeStruct(gra...  95.1 us
    unnamed x6, local copies, waits for them, and re-layouts  4.56 us

profile of v9, /device:TPU:6, one launch (start us, length us, event | category | flops | bytes accessed | tf_op | source)
XLA Modules:
  0.0 100.3 jit_solution(4543989761656182802)
XLA Ops:
  0.6 0.0 copy-start
  0.6 1.4 %copy-done = f32[32,12,1024]{2,0,1:T(8,128)S(1)} copy-done((f32[32,12,1024]{2,0,1:T(8,128)S(1)}, f32[32,12,1024]{2,0,1:T(8,128)}, u32[]{:S(2)}) %copy-start) | copy-done | bytes 1572888
  2.0 0.0 copy-start.1
  2.0 1.1 %copy-done.1 = bf16[32,12,1024]{2,0,1:T(8,128)(2,1)S(1)} copy-done((bf16[32,12,1024]{2,0,1:T(8,128)(2,1)S(1)}, bf16[32,12,1024]{2,0,1:T(8,128)(2,1)}, u32[]{:S(2)}) %copy-start.1) | copy-done | bytes 786456
  3.2 95.1 %shard_map.41 = (bf16[12,32,1024]{2,1,0:T(8,128)(2,1)S(1)}, f32[12,32,1024]{2,1,0:T(8,128)S(1)}) custom-call(bf16[12,32,1024]{2,1,0:T(8,128)(2,1)S(1)} %bitcast.7, f32[12,32,1024]{2,1,0:T(8,128)S(1)} %bitcast.6), custom_call_target="tpu_custom_call" | custom-call | flops 4831838208 | bytes 3145728 | tf_op jit(solution)/shard_map/pallas_call | solution.py:339
  98.2 0.9 copy.6
  99.1 1.1 %copy.7 = f32[32,12,1024]{2,0,1:T(8,128)} copy(f32[32,12,1024]{2,0,1:T(8,128)S(1)} %bitcast.4) | data formatting | bytes 3145728
Async XLA Ops:
  0.6 1.4 %copy-start = (f32[32,12,1024]{2,0,1:T(8,128)S(1)}, f32[32,12,1024]{2,0,1:T(8,128)}, u32[]{:S(2)}) copy-start(f32[32,12,1024]{2,0,1:T(8,128)} %param.3) | copy-start | bytes 4718596
  2.0 1.1 %copy-start.1 = (bf16[32,12,1024]{2,0,1:T(8,128)(2,1)S(1)}, bf16[32,12,1024]{2,0,1:T(8,128)(2,1)}, u32[]{:S(2)}) copy-start(bf16[32,12,1024]{2,0,1:T(8,128)(2,1)} %param.2) | copy-start | bytes 2359300

commit v10 on v9

--- a/solution.py
+++ b/solution.py
@@ -27,6 +27,7 @@
 SPLITS = ROWS // REST
 SIDES_Y = 4
 BATCHES = 4
+VMEM_MIB = 53
 MESH_ID = pl.DeviceIdType.MESH
 
 
@@ -76,10 +77,12 @@
 
 def kernel(
     n_dp,
+    grads_hbm,
+    mom_hbm,
+    out_ref,
+    new_mom_hbm,
     grads_ref,
     mom_ref,
-    out_ref,
-    new_mom_ref,
     rows32,
     sent,
     landed,
@@ -95,6 +98,8 @@
     landed_sem,
     away_sem,
     home_sem,
+    read_sem,
+    write_sem,
 ):
     n_z = n_dp // SIDES_Y
     mats = n_dp // 2
@@ -127,6 +132,20 @@
     def owner_of(matrix):
         return (core + 2 * (matrix // n_z)) * n_z + matrix % n_z
 
+    def read(i):
+        yield pltpu.make_async_copy(mom_hbm.at[i], mom_ref.at[i], read_sem.at[0, i])
+        yield pltpu.make_async_copy(grads_hbm.at[i], grads_ref.at[i], read_sem.at[1, i])
+
+    def write(i):
+        return pltpu.make_async_copy(mom_ref.at[i], new_mom_hbm.at[i], write_sem.at[i])
+
+    def start_read(i, c):
+        for copy in read(i):
+            copy.start()
+        return c
+
+    lax.fori_loop(0, ROWS, start_read, 0)
+
     barrier = pltpu.get_barrier_semaphore()
 
     def greet_owner(i, c):
@@ -150,9 +169,12 @@
         lax.fori_loop(0, mats, greet_rest, 0)
 
     def momentum_row(i, c):
+        for copy in read(i):
+            copy.wait()
         gradient = grads_ref[i].astype(jnp.float32)
         momentum = MOMENT * mom_ref[i] + gradient
-        new_mom_ref[i] = momentum
+        mom_ref[i] = momentum
+        write(i).start()
         nesterov = gradient + MOMENT * momentum
         here = pl.ds(pl.multiple_of(i * mats, 8), mats)
         for tile in range(D // LANES):
@@ -305,6 +327,7 @@
     lax.fori_loop(0, mats, take_home, 0)
 
     def update_row(i, c):
+        write(i).wait()
         here = pl.ds(pl.multiple_of(i * mats, 8), mats)
         for tile in range(D // LANES):
             columns = slice(LANES * tile, LANES * (tile + 1))
@@ -342,9 +365,14 @@
             jax.ShapeDtypeStruct(grads.shape, jnp.bfloat16),
             jax.ShapeDtypeStruct(grads.shape, jnp.float32),
         ],
-        in_specs=[pl.BlockSpec(memory_space=pltpu.VMEM)] * 2,
-        out_specs=[pl.BlockSpec(memory_space=pltpu.VMEM)] * 2,
+        in_specs=[pl.BlockSpec(memory_space=pltpu.HBM)] * 2,
+        out_specs=[
+            pl.BlockSpec(memory_space=pltpu.VMEM),
+            pl.BlockSpec(memory_space=pltpu.HBM),
+        ],
         scratch_shapes=[
+            pltpu.VMEM(grads.shape, jnp.bfloat16),
+            pltpu.VMEM(grads.shape, jnp.float32),
             pltpu.VMEM((D // LANES, ROWS * mats, LANES), jnp.float32),
             packed(mats),
             packed(n_dp),
@@ -360,9 +388,11 @@
             pltpu.SemaphoreType.DMA((n_dp,)),
             pltpu.SemaphoreType.DMA((n_dp,)),
             pltpu.SemaphoreType.DMA((mats,)),
+            pltpu.SemaphoreType.DMA((2, ROWS)),
+            pltpu.SemaphoreType.DMA((ROWS,)),
         ],
         compiler_params=pltpu.CompilerParams(
-            collective_id=0, has_side_effects=True, vmem_limit_bytes=40 * 1024 * 1024
+            collective_id=0, has_side_effects=True, vmem_limit_bytes=VMEM_MIB * 1024 * 1024
         ),
         cost_estimate=pl.CostEstimate(
             flops=8 * height * height * D, bytes_accessed=8 * grads.size, transcendentals=0

time: 102 us -> 100 us (0.980)
  local copies, waits for them, and re-layouts: 4.56 us -> 2.83 us
    unnamed x6 -> x4, local copies, waits for them, and re-layouts: 4.56 us -> 2.83 us
where the time goes in v10:
time: 100 us; the launch traced here: 98.9 us
  Pallas kernels  95.5 us (96%)
  local copies, waits for them, and re-layouts  2.83 us (3%)
    pallas_call x1, Pallas kernels, orthogonalized(): pl.pallas_call(partial(kernel, n_dp), out_shape=[jax.ShapeDtypeStruct(gra...  95.5 us
    unnamed x4, local copies, waits for them, and re-layouts  2.83 us

profile of v10, /device:TPU:6, one launch (start us, length us, event | category | flops | bytes accessed | tf_op | source)
XLA Modules:
  0.0 98.9 jit_solution(7303259244697591568)
XLA Ops:
  0.6 95.5 %shard_map.41 = (bf16[12,32,1024]{2,1,0:T(8,128)(2,1)S(1)}, f32[12,32,1024]{2,1,0:T(8,128)}) custom-call(bf16[12,32,1024]{2,1,0:T(8,128)(2,1)} %bitcast.7, f32[12,32,1024]{2,1,0:T(8,128)} %bitcast.6), custom_call_target="tpu_custom_call" | custom-call | flops 4831838208 | bytes 3145728 | tf_op jit(solution)/shard_map/pallas_call | solution.py:362
  96.1 0.0 copy-start
  96.1 0.9 copy.6
  97.0 0.8 copy-done
  97.8 1.1 %copy.7 = f32[32,12,1024]{2,0,1:T(8,128)} copy(f32[32,12,1024]{2,0,1:T(8,128)S(1)} %bitcast.5) | data formatting | bytes 3145728
Async XLA Ops:
  96.1 1.7 %copy-start = (f32[12,32,1024]{2,1,0:T(8,128)S(1)}, f32[12,32,1024]{2,1,0:T(8,128)}, u32[]{:S(2)}) copy-start(f32[12,32,1024]{2,1,0:T(8,128)} %get-tuple-element.5) | copy-start | bytes 4718596
